TPU v7x, 32 devices: a whole 2x2x4 slice. The times are simulated.
32 devices in a mesh: slab: 8 (over y, x, core), band: 4 (over z).
Axes of the slice: x: 2, y: 2, z: 4, core: 2. Of those that a mesh axis runs over, the one named last changes fastest.
Arguments:
- orbitals: float32 [16, 32, 128, 512], P('slab', None, None, 'band'), may hold values from -6 to 6
- potential: float32 [16, 32, 128], P('slab'), may hold values from -1.5 to 1.5
- projector: float32 [4096, 4, 128], P('slab'), may hold values from -0.1875 to 0.1875
- strength: float32 [512, 4], P('slab'), may hold values from 2 to 20
- entry_slot: int32 [4096], P('slab'), may hold values from 0 to 191
- entry_block: int32 [4096], P('slab'), may hold values from 0 to 63
- entry_count: int32 [8], P('slab'), may hold values from 64 to 512, as said below
Outputs:
- applied: float32 [16, 32, 128, 512], P('slab', None, None, 'band')
- correlation: float32 [512, 512], P(None, 'band')
- subspace: float32 [512, 512], P(None, 'band')
Inputs may be any that keep to these rules, and one draw needn't show every extreme that they name: `entry_count`: entries of a slab's list beyond its count are not part of the problem; at least one slab's list is full.
All inputs are finite; a program needn't handle non-finite values.
Results may differ from a plain program's by a relative error of at most 0.0003.
Values sent between devices are 32-bit elements; how exact they have to be, the bound alone decides.
A program may use at most 192 MiB of HBM per device.

v0:
```python
import jax
import jax.numpy as jnp
from jax import lax
from jax.sharding import PartitionSpec as P

centre_coef = -2.5
near_coef = 4.0 / 3.0
far_coef = -1.0 / 12.0
highest = lax.Precision.HIGHEST


def with_halo(x, sides, width):
    for axis, dim in sides:
        size, length = (lax.axis_size(axis), x.shape[dim])
        up = [(i, (i + 1) % size) for i in range(size)]
        down = [(j, i) for i, j in up]
        last = lax.slice_in_dim(x, length - width, length, axis=dim)
        initial = lax.slice_in_dim(x, 0, width, axis=dim)
        before = lax.ppermute(last, axis, up)
        after = lax.ppermute(initial, axis, down)
        x = jnp.concatenate([before, x, after], axis=dim)
    return x


def local(orbitals, potential, projector, strength, entry_slot, entry_block, entry_count):
    planes, height, row_len, band_cols = orbitals.shape
    padded = with_halo(orbitals, (("slab", 0),), 2)
    laplace = 3.0 * centre_coef * orbitals
    for axis_num in (1, 2):
        laplace = laplace + near_coef * (
            jnp.roll(orbitals, 1, axis_num) + jnp.roll(orbitals, -1, axis_num)
        )
        laplace = laplace + far_coef * (
            jnp.roll(orbitals, 2, axis_num) + jnp.roll(orbitals, -2, axis_num)
        )
    laplace = laplace + near_coef * (padded[3 : 3 + planes] + padded[1 : 1 + planes])
    laplace = laplace + far_coef * (padded[4 : 4 + planes] + padded[0:planes])
    local_part = -0.5 * laplace + potential[..., None] * orbitals
    grid_rows = orbitals.reshape(planes * height, row_len, band_cols)
    entries = entry_slot.shape[0]
    tile_len = min(128, entries)
    atom_slots, channels = strength.shape
    live_count = entry_count[0]
    turns = (live_count + tile_len - 1) // tile_len
    sections = lax.broadcasted_iota(jnp.int32, (3 * atom_slots, tile_len), 0)

    def tile_data(turn_index):
        first = turn_index * tile_len
        slot_ids = lax.dynamic_slice_in_dim(entry_slot, first, tile_len, 0)
        block_ids = lax.dynamic_slice_in_dim(entry_block, first, tile_len, 0)
        values = lax.dynamic_slice_in_dim(projector, first, tile_len, 0)
        positions = first + jnp.arange(tile_len, dtype=jnp.int32)
        onehot = ((slot_ids[None, :] == sections) & (positions < live_count)[None, :]).astype(
            jnp.float32
        )
        return (block_ids, values, onehot)

    def project_step(turn_index, partial_value):
        block_ids, values, onehot = tile_data(turn_index)
        picked = grid_rows[block_ids]
        products = jnp.einsum("epc,eco->epo", values, picked, precision=highest)
        return partial_value + jnp.einsum("se,epo->spo", onehot, products, precision=highest)

    partial_value = lax.fori_loop(
        0, turns, project_step, jnp.zeros((3 * atom_slots, channels, band_cols), jnp.float32)
    )
    padded_partial = with_halo(
        partial_value.reshape(3, atom_slots, channels, band_cols), (("slab", 0),), 1
    )
    coefficient = padded_partial[2] + padded_partial[0] + padded_partial[4]
    scaled = strength[:, :, None] * coefficient
    beside_all = with_halo(scaled[None], (("slab", 0),), 1).reshape(
        3 * atom_slots, channels, band_cols
    )

    def apply_step(turn_index, result):
        block_ids, values, onehot = tile_data(turn_index)
        coef_entry = jnp.einsum("se,spo->epo", onehot, beside_all, precision=highest)
        contrib = jnp.einsum("epc,epo->eco", values, coef_entry, precision=highest)
        return result.at[block_ids].add(contrib)

    sphere_rows = lax.fori_loop(0, turns, apply_step, jnp.zeros_like(grid_rows))
    applied = local_part + sphere_rows.reshape(orbitals.shape)
    grid_cells = orbitals.reshape(-1, band_cols)
    image_rows = applied.reshape(-1, band_cols)
    volume = 1.0 / (lax.axis_size("slab") * planes * height * row_len)
    contract = (((0,), (0,)), ((), ()))
    shard_piece = lax.all_gather(orbitals, "band", axis=3, tiled=True)
    flat_piece = shard_piece.reshape(-1, shard_piece.shape[3])
    over_rows = lax.dot_general(
        flat_piece, grid_cells, contract, precision=highest, preferred_element_type=jnp.float32
    )
    sub_rows = lax.dot_general(
        flat_piece, image_rows, contract, precision=highest, preferred_element_type=jnp.float32
    )
    over_part = over_rows * volume
    sub_part = sub_rows * volume
    correlation, subspace = lax.psum((over_part, sub_part), "slab")
    return (applied, correlation, subspace)


def solution(mesh):
    in_specs = (
        P("slab", None, None, "band"),
        P("slab", None, None),
        P("slab", None, None),
        P("slab", None),
        P("slab"),
        P("slab"),
        P("slab"),
    )
    out_specs = (P("slab", None, None, "band"), P(None, "band"), P(None, "band"))
    return jax.shard_map(local, mesh=mesh, in_specs=in_specs, out_specs=out_specs, check_vma=False)
```

profile of v0, /device:TPU:0, one launch (start us, length us, event | category | flops | bytes accessed | tf_op | source)
XLA Modules:
  0.0 426.0 jit_solution(8113622959580461318)
XLA Ops:
  7.2 5.6 %copy.11 = f32[2,32,128,128]{2,3,1,0:T(8,128)} copy(f32[2,32,128,128]{3,2,1,0:T(8,128)} %param.11) | data formatting | bytes 8388608 | tf_op args[0]
  12.9 3.4 collective-permute-start
  17.1 70.3 %while.22 = (s32[]{:T(128)}, f32[192,4,128]{2,0,1:T(8,128)S(1)}, s32[]{:T(128)}, s32[512]{0:T(512)S(1)}, s32[]{:T(128)}, /*index=5*/f32[512,4,128]{2,1,0:T(4,128...) while((s32[]{:T(128)}, f32[192,4,128]{2,0,1:T(8,128)S(1)}, ...), condition=%wide.region_1.2_spmd.clone, body=%wide.region_0.1_spmd.clone.sunk | while | flops 251807360 | bytes 26746808 | solution.py:64
  17.2 7.1 %gather_fusion = f32[128,128,128]{2,1,0:T(8,128)} fusion(f32[64,128,128]{2,1,0:T(8,128)} %get-tuple-element.325, s32[1024]{0:T(1024)S(1)} %pad_clamp_fusion.2), kind=kCustom, calls=%fused_computation.clone.clone.1 | custom fusion | bytes 16777728 | tf_op jit(solution)/shard_map/while/body/gather | solution.py:60
  24.3 10.1 %fusion.72 = f32[128,4,128]{2,1,0:T(4,128)S(1)} fusion(f32[128,128,128]{2,1,0:T(8,128)} %gather_fusion, f32[512,4,128]{2,1,0:T(4,128)S(1)} %get-tuple-element.323, s32[]{:T(128)S(6)} %select_n.33), kind=kOutput, calls=%fused_computation.6.clone.1 | convolution fusion | flops 100663296 | bytes 8912900 | tf_op jit(solution)/shard_map/while/body/epc,eco->epo/dot_general | solution.py:61
  35.8 6.5 %gather_fusion = f32[128,128,128]{2,1,0:T(8,128)} fusion(f32[64,128,128]{2,1,0:T(8,128)} %get-tuple-element.325, s32[1024]{0:T(1024)S(1)} %pad_clamp_fusion.2), kind=kCustom, calls=%fused_computation.clone.clone.1 | custom fusion | bytes 16777728 | tf_op jit(solution)/shard_map/while/body/gather | solution.py:60
  42.3 9.4 %fusion.72 = f32[128,4,128]{2,1,0:T(4,128)S(1)} fusion(f32[128,128,128]{2,1,0:T(8,128)} %gather_fusion, f32[512,4,128]{2,1,0:T(4,128)S(1)} %get-tuple-element.323, s32[]{:T(128)S(6)} %select_n.33), kind=kOutput, calls=%fused_computation.6.clone.1 | convolution fusion | flops 100663296 | bytes 8912900 | tf_op jit(solution)/shard_map/while/body/epc,eco->epo/dot_general | solution.py:61
  53.0 6.5 %gather_fusion = f32[128,128,128]{2,1,0:T(8,128)} fusion(f32[64,128,128]{2,1,0:T(8,128)} %get-tuple-element.325, s32[1024]{0:T(1024)S(1)} %pad_clamp_fusion.2), kind=kCustom, calls=%fused_computation.clone.clone.1 | custom fusion | bytes 16777728 | tf_op jit(solution)/shard_map/while/body/gather | solution.py:60
  59.6 9.4 %fusion.72 = f32[128,4,128]{2,1,0:T(4,128)S(1)} fusion(f32[128,128,128]{2,1,0:T(8,128)} %gather_fusion, f32[512,4,128]{2,1,0:T(4,128)S(1)} %get-tuple-element.323, s32[]{:T(128)S(6)} %select_n.33), kind=kOutput, calls=%fused_computation.6.clone.1 | convolution fusion | flops 100663296 | bytes 8912900 | tf_op jit(solution)/shard_map/while/body/epc,eco->epo/dot_general | solution.py:61
  70.3 6.5 %gather_fusion = f32[128,128,128]{2,1,0:T(8,128)} fusion(f32[64,128,128]{2,1,0:T(8,128)} %get-tuple-element.325, s32[1024]{0:T(1024)S(1)} %pad_clamp_fusion.2), kind=kCustom, calls=%fused_computation.clone.clone.1 | custom fusion | bytes 16777728 | tf_op jit(solution)/shard_map/while/body/gather | solution.py:60
  76.8 9.4 %fusion.72 = f32[128,4,128]{2,1,0:T(4,128)S(1)} fusion(f32[128,128,128]{2,1,0:T(8,128)} %gather_fusion, f32[512,4,128]{2,1,0:T(4,128)S(1)} %get-tuple-element.323, s32[]{:T(128)S(6)} %select_n.33), kind=kOutput, calls=%fused_computation.6.clone.1 | convolution fusion | flops 100663296 | bytes 8912900 | tf_op jit(solution)/shard_map/while/body/epc,eco->epo/dot_general | solution.py:61
  87.5 2.6 collective-permute-start.3
  92.2 7.5 %fusion.48 = (f32[2,30,128,128]{3,2,1,0:T(8,128)}, f32[2,30,128,128]{3,2,1,0:T(8,128)}) fusion(f32[2,32,128,128]{3,2,1,0:T(8,128)} %bitcast.51), kind=kLoop, calls=%fused_computation.66 | loop fusion | bytes 15728640 | tf_op jit(solution)/shard_map/jit(_roll_static)/slice | solution.py:34
  99.8 4.2 fusion.50
  104.0 4.1 fusion.44
  108.1 4.1 fusion.46
  112.5 2.6 collective-permute-start.5
  115.2 3.8 collective-permute-done.4
  119.3 2.5 broadcast_in_dim.11
  121.8 171.6 %while.23 = (s32[]{:T(128)}, f32[64,128,128]{2,1,0:T(8,128)}, s32[]{:T(128)}, s32[512]{0:T(512)S(1)}, f32[512,4,128]{2,1,0:T(4,128)S(1)}, /*index=5*/s32[512]{0:...) while((s32[]{:T(128)}, f32[64,128,128]{2,1,0:T(8,128)}, ...), condition=%wide.region_4.5_spmd.clone, body=%wide.region_2.4_spmd.clone.sunk | while | flops 253805184 | bytes 34737592 | solution.py:82
  123.1 15.4 %fusion.78 = f32[128,128,128]{2,1,0:T(8,128)} fusion(f32[128,4,128]{2,0,1:T(8,128)S(1)} %fusion.77, f32[512,4,128]{2,1,0:T(4,128)S(1)} %get-tuple-element.358, s32[]{:T(128)S(6)} %select_n.35), kind=kOutput, calls=%fused_computation.19.clone.1 | convolution fusion | flops 100663296 | bytes 8912900 | tf_op jit(solution)/shard_map/while/body/epc,epo->eco/dot_general | solution.py:79
  138.7 26.1 %scatter_fusion = f32[64,128,128]{2,1,0:T(8,128)} fusion(f32[64,128,128]{2,1,0:T(8,128)} %get-tuple-element.343, s32[128]{0:T(128)S(1)} %compare_select_fusion.5, f32[128,128,128]{2,1,0:T(8,128)} %fusion.78), kind=kCustom, calls=%fused_computation.1.clone.clone.1 | custom fusion | flops 2097152 | bytes 25166336 | tf_op jit(solution)/shard_map/while/body/scatter-add | solution.py:80
  165.9 15.4 %fusion.78 = f32[128,128,128]{2,1,0:T(8,128)} fusion(f32[128,4,128]{2,0,1:T(8,128)S(1)} %fusion.77, f32[512,4,128]{2,1,0:T(4,128)S(1)} %get-tuple-element.358, s32[]{:T(128)S(6)} %select_n.35), kind=kOutput, calls=%fused_computation.19.clone.1 | convolution fusion | flops 100663296 | bytes 8912900 | tf_op jit(solution)/shard_map/while/body/epc,epo->eco/dot_general | solution.py:79
  181.4 26.4 %scatter_fusion = f32[64,128,128]{2,1,0:T(8,128)} fusion(f32[64,128,128]{2,1,0:T(8,128)} %get-tuple-element.343, s32[128]{0:T(128)S(1)} %compare_select_fusion.5, f32[128,128,128]{2,1,0:T(8,128)} %fusion.78), kind=kCustom, calls=%fused_computation.1.clone.clone.1 | custom fusion | flops 2097152 | bytes 25166336 | tf_op jit(solution)/shard_map/while/body/scatter-add | solution.py:80
  208.9 15.4 %fusion.78 = f32[128,128,128]{2,1,0:T(8,128)} fusion(f32[128,4,128]{2,0,1:T(8,128)S(1)} %fusion.77, f32[512,4,128]{2,1,0:T(4,128)S(1)} %get-tuple-element.358, s32[]{:T(128)S(6)} %select_n.35), kind=kOutput, calls=%fused_computation.19.clone.1 | convolution fusion | flops 100663296 | bytes 8912900 | tf_op jit(solution)/shard_map/while/body/epc,epo->eco/dot_general | solution.py:79
  224.4 26.2 %scatter_fusion = f32[64,128,128]{2,1,0:T(8,128)} fusion(f32[64,128,128]{2,1,0:T(8,128)} %get-tuple-element.343, s32[128]{0:T(128)S(1)} %compare_select_fusion.5, f32[128,128,128]{2,1,0:T(8,128)} %fusion.78), kind=kCustom, calls=%fused_computation.1.clone.clone.1 | custom fusion | flops 2097152 | bytes 25166336 | tf_op jit(solution)/shard_map/while/body/scatter-add | solution.py:80
  251.7 15.4 %fusion.78 = f32[128,128,128]{2,1,0:T(8,128)} fusion(f32[128,4,128]{2,0,1:T(8,128)S(1)} %fusion.77, f32[512,4,128]{2,1,0:T(4,128)S(1)} %get-tuple-element.358, s32[]{:T(128)S(6)} %select_n.35), kind=kOutput, calls=%fused_computation.19.clone.1 | convolution fusion | flops 100663296 | bytes 8912900 | tf_op jit(solution)/shard_map/while/body/epc,epo->eco/dot_general | solution.py:79
  267.2 26.2 %scatter_fusion = f32[64,128,128]{2,1,0:T(8,128)} fusion(f32[64,128,128]{2,1,0:T(8,128)} %get-tuple-element.343, s32[128]{0:T(128)S(1)} %compare_select_fusion.5, f32[128,128,128]{2,1,0:T(8,128)} %fusion.78), kind=kCustom, calls=%fused_computation.1.clone.clone.1 | custom fusion | flops 2097152 | bytes 25166336 | tf_op jit(solution)/shard_map/while/body/scatter-add | solution.py:80
  293.4 21.8 %fusion.30 = f32[2,32,128,128]{3,2,1,0:T(8,128)} fusion(f32[2,32,128,128]{3,2,1,0:T(8,128)} %bitcast.59, f32[2,32,128,128]{3,2,1,0:T(8,128)} %bitcast.52, f32[2,32,128,128]{3,2,1,0:T(8,128)} %collective-permute-done.1, f32[2,32,128,128]{3,2,1,0:T(8,128)} %collective-permute-done, f32[2,31,128,128]{3,2,1,0:T(8,128)} %get-tuple-element.189, ...), kind=kLoop, calls=%fused_computation.37 | loop fusion | flops 34603008 | bytes 54558720 | tf_op jit(solution)/shard_map/add | solution.py:83
  315.3 27.4 %fusion.41 = f32[512,128]{1,0:T(8,128)} fusion(f32[2,32,128,512]{2,3,1,0:T(8,128)} %all-gather.2.cloned.1.call-done, f32[2,32,128,128]{3,2,1,0:T(8,128)} %bitcast.53), kind=kOutput, calls=%fused_computation.55 | convolution fusion | flops 6442516480 | bytes 21233664 | tf_op jit(solution)/shard_map/dot_general | solution.py:90
  342.8 18.5 %fusion.40 = f32[512,128]{0,1:T(8,128)} fusion(f32[2,32,128,128]{3,2,1,0:T(8,128)S(1)} %copy-done.2, f32[2,32,128,512]{2,3,1,0:T(8,128)S(1)} %copy-done.1), kind=kOutput, calls=%fused_computation.53 | convolution fusion | flops 6442516480 | bytes 21233664 | tf_op jit(solution)/shard_map/dot_general | solution.py:93
  361.3 54.2 %all-reduce.3.cloned.1.call-done = (f32[512,128]{1,0:T(8,128)}, f32[512,128]{0,1:T(8,128)}) async-done(((f32[512,128]{1,0:T(8,128)}, f32[512,128]{0,1:T(8,128)}), (f32[512,128]{1,0:T(8,128)}, f32[512,128]{0,1:T(8,128)})) %all-reduce.3.cloned.1.call-update) | async-done | bytes 524304 | tf_op jit(solution)/shard_map/psum | solution.py:98
  (76 shorter events, 16.0 us)
Async XLA Ops:
  7.2 308.1 %all-gather.2.cloned.1.call-start = ((), (), s32[]{:S(2)}) async-start(), calls=%async_computation | async-start | bytes 20971520 | tf_op jit(solution)/shard_map/all_gather | solution.py:88
  12.9 4.2 copy-start.3
  12.9 4.2 copy-start.6
  12.9 4.2 copy-start.7
  12.9 402.6 %all-reduce.3.cloned.1.call-start = ((), (), s32[]{:S(2)}) async-start(), calls=%async_computation.1 | async-start | bytes 1048576 | tf_op jit(solution)/shard_map/psum | solution.py:98
  12.9 280.5 %collective-permute-start = (f32[2,32,128,128]{3,2,1,0:T(8,128)}, f32[2,32,128,128]{3,2,1,0:T(8,128)}, u32[]{:S(2)}, u32[]{:S(2)}) collective-permute-start(f32[2,32,128,128]{3,2,1,0:T(8,128)} %param.11), channel_id=1, source_target_pairs={{4,0},{8,4},{12,8},{16,12},{20,16},{24,20},{28,24},{0,28},{5,1},{9... | collective-permute-start | bytes 12582920 | tf_op jit(solution)/shard_map/ppermute | solution.py:20
  16.3 277.1 %collective-permute-start.1 = (f32[2,32,128,128]{3,2,1,0:T(8,128)}, f32[2,32,128,128]{3,2,1,0:T(8,128)}, u32[]{:S(2)}, u32[]{:S(2)}) collective-permute-start(f32[2,32,128,128]{3,2,1,0:T(8,128)} %param.11), channel_id=1, source_target_pairs={{0,4},{4,8},{8,12},{12,16},{16,20},{20,24},{24,28},{28,0},{1,5},{5... | collective-permute-start | bytes 12582920 | tf_op jit(solution)/shard_map/ppermute | solution.py:19
  87.4 24.9 %collective-permute-start.2 = (f32[1,64,4,128]{3,1,2,0:T(8,128)S(1)}, f32[1,64,4,128]{3,1,2,0:T(8,128)S(1)}, u32[]{:S(2)}, u32[]{:S(2)}) collective-permute-start(f32[1,64,4,128]{3,1,2,0:T(8,128)S(1)} %get-tuple-element.192), channel_id=1, source_target_pairs={{0,4},{4,8},{8,12},{12,16},{16,20},{20,24},{24,28},{28,0},{1,5},{5... | collective-permute-start | bytes 393224 | tf_op jit(solution)/shard_map/ppermute | solution.py:19
  87.5 24.8 %collective-permute-start.3 = (f32[1,64,4,128]{3,1,2,0:T(8,128)S(1)}, f32[1,64,4,128]{3,1,2,0:T(8,128)S(1)}, u32[]{:S(2)}, u32[]{:S(2)}) collective-permute-start(f32[1,64,4,128]{3,1,2,0:T(8,128)S(1)} %get-tuple-element.193), channel_id=1, source_target_pairs={{4,0},{8,4},{12,8},{16,12},{20,16},{24,20},{28,24},{0,28},{5,1},{9... | collective-permute-start | bytes 393224 | tf_op jit(solution)/shard_map/ppermute | solution.py:20
  92.2 7.6 %copy-start = (f32[64,128,128]{2,1,0:T(8,128)S(1)}, f32[64,128,128]{2,1,0:T(8,128)}, u32[]{:S(2)}) copy-start(f32[64,128,128]{2,1,0:T(8,128)} %get-tuple-element.376) | copy-start | bytes 12582916
  108.1 4.2 copy-start.5
  112.4 6.5 %collective-permute-start.4 = (f32[1,64,4,128]{3,1,2,0:T(8,128)S(1)}, f32[1,64,4,128]{3,1,2,0:T(8,128)S(1)}, u32[]{:S(2)}, u32[]{:S(2)}) collective-permute-start(f32[1,64,4,128]{3,1,2,0:T(8,128)S(1)} %fusion.43), channel_id=1, source_target_pairs={{0,4},{4,8},{8,12},{12,16},{16,20},{20,24},{24,28},{28,0},{1,5},{5... | collective-permute-start | bytes 393224 | tf_op jit(solution)/shard_map/ppermute | solution.py:19
  112.5 6.5 %collective-permute-start.5 = (f32[1,64,4,128]{3,1,2,0:T(8,128)S(1)}, f32[1,64,4,128]{3,1,2,0:T(8,128)S(1)}, u32[]{:S(2)}, u32[]{:S(2)}) collective-permute-start(f32[1,64,4,128]{3,1,2,0:T(8,128)S(1)} %fusion.43), channel_id=1, source_target_pairs={{4,0},{8,4},{12,8},{16,12},{20,16},{24,20},{28,24},{0,28},{5,1},{9... | collective-permute-start | bytes 393224 | tf_op jit(solution)/shard_map/ppermute | solution.py:20
  121.8 171.6 %copy-start.4 = (f32[2,32,128]{2,1,0:T(8,128)S(1)}, f32[2,32,128]{2,1,0:T(8,128)}, u32[]{:S(2)}) copy-start(f32[2,32,128]{2,1,0:T(8,128)} %param.12) | copy-start | bytes 98308
  315.3 27.5 %copy-start.1 = (f32[2,32,128,512]{2,3,1,0:T(8,128)S(1)}, f32[2,32,128,512]{2,3,1,0:T(8,128)}, u32[]{:S(2)}) copy-start(f32[2,32,128,512]{2,3,1,0:T(8,128)} %all-gather.2.cloned.1.call-done) | copy-start | bytes 50331652
  315.3 27.5 %copy-start.2 = (f32[2,32,128,128]{3,2,1,0:T(8,128)S(1)}, f32[2,32,128,128]{3,2,1,0:T(8,128)}, u32[]{:S(2)}) copy-start(f32[2,32,128,128]{3,2,1,0:T(8,128)} %fusion.30) | copy-start | bytes 12582916
Sparse Core Ops, SparseCore 0:
  13.0 289.5 all-gather.1
  361.4 54.0 all-reduce.2
where the time goes:
time: 430 us; the launch traced here: 426 us
  matrix products  149 us (35%)
  other arithmetic  133 us (31%)
  local copies, waits for them, and re-layouts  61.5 us (14%)
  waiting for transfers between devices  58 us (13%)
  between operations  15.1 us (4%)
  starting transfers between devices  8.85 us (2%)
    scatter-add x4, other arithmetic, apply_step(): return result.at[block_ids].add(contrib)  105 us
    dot_general x4, matrix products, apply_step(): contrib = jnp.einsum('epc,epo->eco', values, coef_entry, precision=highest)  61.7 us
    psum x1, waiting for transfers between devices, local(): correlation, subspace = lax.psum((over_part, sub_part), 'slab')  54.2 us
    dot_general x4, matrix products, project_step(): products = jnp.einsum('epc,eco->epo', values, picked, precision=highest)  38.3 us
    dot_general x1, matrix products, local(): lax.dot_general(flat_piece, grid_cells, contract, precision=highest, pref...  27.4 us
    gather x4, local copies, waits for them, and re-layouts, project_step(): picked = grid_rows[block_ids]  26.8 us
    add x1, other arithmetic, local(): applied = local_part + sphere_rows.reshape(orbitals.shape)  21.8 us
    dot_general x1, matrix products, local(): lax.dot_general(flat_piece, image_rows, contract, precision=highest, pref...  18.5 us
  transfers between devices with their start and end apart: 8, of which 2 were waited for; matrix products, arithmetic and copies ran while one was open for 68% of the time, Pallas kernels for 0%

commit v1 on v0

v1 whole, which is shorter than its diff:
```python
import functools

import jax
import jax.numpy as jnp
from jax import lax
from jax.experimental import pallas as pl
from jax.experimental.pallas import tpu as pltpu
from jax.sharding import PartitionSpec as P

centre_coef = -2.5
near_coef = 4.0 / 3.0
far_coef = -1.0 / 12.0
highest = lax.Precision.HIGHEST
MIB = 1 << 20

first_round = ((0, 3), (3, 1), (1, 2), (2, 0))
second_round = ((0, 1), (3, 2))


def project_kernel(slots, slot_ref, block_ref, count_ref, projector_ref, x_ref, w_ref, part_ref):
    rows = x_ref.shape[0]
    channels = projector_ref.shape[1]

    @pl.loop(0, rows)
    def _(row):
        w_ref[row] = jnp.zeros(w_ref.shape[1:], jnp.float32)

    @pl.loop(0, count_ref[0])
    def _(entry):
        slot = slot_ref[entry]
        row = block_ref[entry]
        for channel in range(channels):
            place = pl.ds(channel * slots + slot, 1)
            w_ref[row, place, :] = (
                w_ref[row, place, :] + projector_ref[entry, pl.ds(channel, 1), :]
            )

    part_ref[...] = jnp.zeros_like(part_ref)

    @pl.loop(0, rows)
    def _(row):
        part_ref[...] += jnp.dot(
            w_ref[row], x_ref[row], precision=highest, preferred_element_type=jnp.float32
        )


def project(entry_slot, entry_block, entry_count, projector, grid_rows, slots):
    rows, cells, cols = grid_rows.shape
    channels = projector.shape[1]
    smem = pl.BlockSpec(memory_space=pltpu.SMEM)
    vmem = pl.BlockSpec(memory_space=pltpu.VMEM)
    return pl.pallas_call(
        functools.partial(project_kernel, slots),
        out_shape=(
            jax.ShapeDtypeStruct((rows, channels * slots, cells), jnp.float32),
            jax.ShapeDtypeStruct((channels * slots, cols), jnp.float32),
        ),
        in_specs=[smem, smem, smem, vmem, vmem],
        out_specs=(vmem, vmem),
        compiler_params=pltpu.CompilerParams(vmem_limit_bytes=48 * MIB),
        cost_estimate=pl.CostEstimate(
            flops=12 * rows * channels * slots * cells * cols,
            bytes_accessed=4 * rows * channels * slots * cells,
            transcendentals=0,
        ),
        name="project",
    )(entry_slot, entry_block, entry_count, projector, grid_rows)


def apply_kernel(x_ref, before_ref, after_ref, potential_ref, scaled_ref, w_ref, out_ref):
    planes, height, cells, cols = x_ref.shape
    y = pl.program_id(0)

    def plane(z, at):
        if z < 0:
            return before_ref[planes + z, at]
        if z >= planes:
            return after_ref[z - planes, at]
        return x_ref[z, at]

    for z in range(planes):
        centre = x_ref[z, y]
        near = plane(z - 1, y) + plane(z + 1, y)
        far = plane(z - 2, y) + plane(z + 2, y)
        near += x_ref[z, lax.rem(y + 1, height)] + x_ref[z, lax.rem(y + height - 1, height)]
        far += x_ref[z, lax.rem(y + 2, height)] + x_ref[z, lax.rem(y + height - 2, height)]
        near += pltpu.roll(centre, 1, 0) + pltpu.roll(centre, cells - 1, 0)
        far += pltpu.roll(centre, 2, 0) + pltpu.roll(centre, cells - 2, 0)
        level = jnp.broadcast_to(potential_ref[z, pl.ds(y, 1), :], (cols, cells)).T
        sphere = lax.dot_general(
            w_ref[z, 0],
            scaled_ref[...],
            (((0,), (0,)), ((), ())),
            precision=highest,
            preferred_element_type=jnp.float32,
        )
        out_ref[z, 0] = (
            (level - 1.5 * centre_coef) * centre
            - 0.5 * near_coef * near
            - 0.5 * far_coef * far
            + sphere
        )


def apply(orbitals, before, after, potential, scaled, weights):
    planes, height, cells, cols = orbitals.shape
    depth = weights.shape[1]
    vmem = pl.BlockSpec(memory_space=pltpu.VMEM)
    return pl.pallas_call(
        apply_kernel,
        grid=(height,),
        out_shape=jax.ShapeDtypeStruct(orbitals.shape, jnp.float32),
        in_specs=[vmem] * 5 + [pl.BlockSpec((planes, 1, depth, cells), lambda y: (0, y, 0, 0))],
        out_specs=pl.BlockSpec((planes, 1, cells, cols), lambda y: (0, y, 0, 0)),
        compiler_params=pltpu.CompilerParams(vmem_limit_bytes=48 * MIB),
        cost_estimate=pl.CostEstimate(
            flops=12 * planes * height * depth * cells * cols,
            bytes_accessed=4 * planes * height * depth * cells,
            transcendentals=0,
        ),
        name="apply",
    )(orbitals, before, after, potential, scaled, weights.reshape(planes, height, depth, cells))


def products(left, orbitals, applied):
    cols = orbitals.shape[-1]
    left = left.reshape(-1, cols)
    contract = (((0,), (0,)), ((), ()))
    return jnp.stack(
        [
            lax.dot_general(
                left,
                right.reshape(-1, cols),
                contract,
                precision=lax.Precision.HIGH,
                preferred_element_type=jnp.float32,
            )
            for right in (orbitals, applied)
        ]
    )


def local(orbitals, potential, projector, strength, entry_slot, entry_block, entry_count):
    planes, height, cells, cols = orbitals.shape
    atom_slots, channels = strength.shape
    slots = 3 * atom_slots
    slabs = lax.axis_size("slab")
    up = [(i, (i + 1) % slabs) for i in range(slabs)]
    down = [(j, i) for i, j in up]
    band = lax.axis_index("band")

    before = lax.ppermute(orbitals, "slab", up)
    after = lax.ppermute(orbitals, "slab", down)
    met_second = lax.ppermute(orbitals, "band", second_round)
    met_first = lax.ppermute(orbitals, "band", first_round)

    weights, partial_value = project(
        entry_slot,
        entry_block,
        entry_count,
        projector,
        orbitals.reshape(planes * height, cells, cols),
        slots,
    )
    partial_value = partial_value.reshape(channels, 3, atom_slots, cols)
    from_left = lax.ppermute(partial_value[:, 2], "slab", up)
    from_right = lax.ppermute(partial_value[:, 0], "slab", down)
    coefficient = partial_value[:, 1] + from_left + from_right
    scaled = strength.T[:, :, None] * coefficient
    beside_all = jnp.stack(
        [lax.ppermute(scaled, "slab", up), scaled, lax.ppermute(scaled, "slab", down)], axis=1
    ).reshape(channels * slots, cols)

    applied = apply(orbitals, before, after, potential, beside_all, weights)

    volume = 1.0 / (slabs * planes * height * cells)
    early = jnp.stack(
        [products(orbitals, orbitals, applied), products(met_second, orbitals, applied)]
    )
    own, second = lax.psum(early * volume, "slab")
    first = lax.psum(products(met_first, orbitals, applied) * volume, "slab")

    def mirror(blocks, pairs):
        return lax.ppermute(
            jnp.swapaxes(blocks, 1, 2), "band", [(there, here) for here, there in pairs]
        )

    second = second + mirror(second, second_round)
    mirrored = mirror(first, first_round)
    found = jnp.stack([own, second, first, mirrored])
    kinds = [[0] * 4 for _ in range(4)]
    for here, there in second_round:
        kinds[here][there] = kinds[there][here] = 1
    for here, there in first_round:
        kinds[there][here] = 2
        kinds[here][there] = 3
    order = jnp.array(kinds, jnp.int32)[band]
    rows = jnp.concatenate(
        [lax.dynamic_index_in_dim(found, order[r], 0, keepdims=False) for r in range(4)], axis=1
    )
    return applied, rows[0], rows[1]


def solution(mesh):
    in_specs = (
        P("slab", None, None, "band"),
        P("slab", None, None),
        P("slab", None, None),
        P("slab", None),
        P("slab"),
        P("slab"),
        P("slab"),
    )
    out_specs = (P("slab", None, None, "band"), P(None, "band"), P(None, "band"))
    return jax.shard_map(local, mesh=mesh, in_specs=in_specs, out_specs=out_specs, check_vma=False)
```

time: 430 us -> 290 us (0.67)
  other arithmetic: 133 us -> 2.54 us
  matrix products: 149 us -> 20.3 us
  Pallas kernels: 0 us -> 79.7 us
  waiting for transfers between devices: 58 us -> 132 us
  local copies, waits for them, and re-layouts: 61.5 us -> 12.3 us
  starting transfers between devices: 8.85 us -> 19.7 us
  between operations: 15.1 us -> 22.6 us
    dot_general x18 -> x6, matrix products: 149 us -> 20.3 us  [products(): lax.dot_general(left, right.reshape(-1, cols), contract, precision=lax.Pr...]
    scatter-add x4 -> x0, other arithmetic: 105 us -> none  [apply_step(): return result.at[block_ids].add(contrib)]
    pallas_call x0 -> x2, Pallas kernels: none -> 79.7 us  [the longest x1 41.4 us: project(): pl.pallas_call(functools.partial(project_kernel, slots), out_shape=(jax.S...]
    ppermute x6 -> x10, waiting for transfers between devices: 3.81 us -> 80.3 us  [the longest x1 45.4 us: local(): from_left = lax.ppermute(partial_value[:, 2], 'slab', up)]
    gather x4 -> x0, local copies, waits for them, and re-layouts: 26.8 us -> none  [project_step(): picked = grid_rows[block_ids]]
    add x1 -> x0, other arithmetic: 21.8 us -> none  [local(): applied = local_part + sphere_rows.reshape(orbitals.shape)]
    slice x9 -> x1, local copies, waits for them, and re-layouts: 22.2 us -> 0.65 us  [local(): order[r]]
    ppermute x6 -> x10, starting transfers between devices: 8.77 us -> 19.7 us  [the longest x2 5.82 us: mirror(): lax.ppermute(jnp.swapaxes(blocks, 1, 2), 'band', [(there, here) for here,...]
  transfers between devices with their start and end apart: 8 -> 11, of which waited for: 2 -> 7; matrix products, arithmetic and copies ran while one was open for 68% -> 6% of each run, Pallas kernels for 0% -> 28%
where the time goes in v1:
time: 290 us; the launch traced here: 289 us
  waiting for transfers between devices  132 us (46%)
  Pallas kernels  79.7 us (27%)
  between operations  22.6 us (8%)
  matrix products  20.3 us (7%)
  starting transfers between devices  19.7 us (7%)
  local copies, waits for them, and re-layouts  12.3 us (4%)
    psum x1, waiting for transfers between devices, local(): first = lax.psum(products(met_first, orbitals, applied) * volume, 'slab')  51.6 us
    ppermute x1, waiting for transfers between devices, local(): from_left = lax.ppermute(partial_value[:, 2], 'slab', up)  45.4 us
    pallas_call x1, Pallas kernels, project(): pl.pallas_call(functools.partial(project_kernel, slots), out_shape=(jax.S...  41.4 us
    pallas_call x1, Pallas kernels, apply(): pl.pallas_call(apply_kernel, grid=(height,), out_shape=jax.ShapeDtypeStru...  38.3 us
    ppermute x1, waiting for transfers between devices, local(): met_first = lax.ppermute(orbitals, 'band', first_round)  27.1 us
    dot_general x6, matrix products, products(): lax.dot_general(left, right.reshape(-1, cols), contract, precision=lax.Pr...  20.3 us
    unnamed x15, local copies, waits for them, and re-layouts  7.92 us
    ppermute x2, starting transfers between devices, mirror(): lax.ppermute(jnp.swapaxes(blocks, 1, 2), 'band', [(there, here) for here,...  5.82 us
  transfers between devices with their start and end apart: 11, of which 7 were waited for; matrix products, arithmetic and copies ran while one was open for 6% of the time, Pallas kernels for 28%

profile of v1, /device:TPU:0, one launch (start us, length us, event | category | flops | bytes accessed | tf_op | source)
XLA Modules:
  0.0 289.0 jit_solution(14774185459142878549)
XLA Ops:
  7.2 5.7 %copy.19 = f32[2,32,128,128]{2,3,1,0:T(8,128)} copy(f32[2,32,128,128]{3,2,1,0:T(8,128)} %x_ref.1) | data formatting | bytes 8388608 | tf_op args[0]
  12.9 5.2 %collective-permute-start.6 = (f32[2,32,128,128]{2,3,1,0:T(8,128)}, f32[2,32,128,128]{2,3,1,0:T(8,128)S(1)}, u32[]{:S(2)}, u32[]{:S(2)}) collective-permute-start(f32[2,32,128,128]{2,3,1,0:T(8,128)} %copy.19), channel_id=1, source_target_pairs={{0,1},{3,2},{4,5},{7,6},{8,9},{11,10},{12,13},{15,14},{16,17},{19,... | collective-permute-start | bytes 12582920 | tf_op jit(solution)/shard_map/ppermute | solution.py:154
  18.2 2.6 collective-permute-start.1
  20.8 2.5 collective-permute-start.8
  24.0 2.2 copy-done
  26.2 41.4 %project.1 = (f32[64,768,128]{2,1,0:T(8,128)}, f32[768,128]{1,0:T(8,128)S(1)}) custom-call(s32[512]{0:T(512)S(1)} %copy-done.3, s32[512]{0:T(512)S(1)} %copy-done.4, s32[1]{0:T(128)S(6)} %copy.49.count_ref, f32[512,4,128]{2,1,0:T(4,128)S(1)} %copy-done.2, f32[64,128,128]{2,1,0:T(8,128)S(1)} %bitcast.108), custom_call_target="tpu_custom_call" | custom-call | flops 9663676416 | bytes 25165824 | tf_op jit(solution)/shard_map/project/pallas_call | solution.py:52
  67.7 45.4 %collective-permute-done.2 = f32[4,64,128]{2,1,0:T(8,128)S(1)} collective-permute-done((f32[4,64,128]{2,1,0:T(8,128)S(1)}, f32[4,64,128]{2,1,0:T(8,128)S(1)}, u32[]{:S(2)}, u32[]{:S(2)}) %collective-permute-start.2) | collective-permute-done | bytes 131104 | tf_op jit(solution)/shard_map/ppermute | solution.py:166
  113.1 2.5 collective-permute-done.3
  115.7 3.1 %collective-permute-start.5 = (f32[4,64,128]{2,1,0:T(8,128)S(1)}, f32[4,64,128]{2,1,0:T(8,128)S(1)}, u32[]{:S(2)}, u32[]{:S(2)}) collective-permute-start(f32[4,64,128]{2,1,0:T(8,128)S(1)} %fusion.2), channel_id=1, source_target_pairs={{4,0},{8,4},{12,8},{16,12},{20,16},{24,20},{28,24},{0,28},{5,1},{9... | collective-permute-start | bytes 393224 | tf_op jit(solution)/shard_map/ppermute | solution.py:171
  118.8 2.5 collective-permute-done.5
  121.4 0.3 collective-permute-start.4
  121.7 3.4 %convolution_bitcast_fusion.5 = f32[1,128,128]{2,1,0:T(8,128)S(1)} fusion(f32[2,32,128,128]{3,2,1,0:T(8,128)S(1)} %copy-done), kind=kOutput, calls=%fused_computation.5 | convolution fusion | flops 805306368 | bytes 4259840 | tf_op jit(solution)/shard_map/dot_general | solution.py:131
  125.1 1.9 collective-permute-done.4
  127.1 2.2 convolution_bitcast_fusion.3
  129.4 38.3 %apply.1 = f32[2,32,128,128]{3,2,1,0:T(8,128)} custom-call(f32[2,32,128,128]{3,2,1,0:T(8,128)S(1)} %copy-done, f32[2,32,128,128]{3,2,1,0:T(8,128)} %collective-permute-done.before_ref, f32[2,32,128,128]{3,2,1,0:T(8,128)} %collective-permute-done.1.after_ref, f32[2,32,128]{2,1,0:T(8,128)S(1)} %copy-done.1, f32[768,128]{1,0:T(8,128)S(1)} %bitcast.109, ...), custom_call_target="tpu_custom_call" | custom-call | flops 9663676416 | bytes 25165824 | tf_op jit(solution)/shard_map/apply/pallas_call | solution.py:109
  167.6 4.4 %convolution_bitcast_fusion.2 = f32[1,128,128]{2,1,0:T(8,128)S(1)} fusion(f32[2,32,128,128]{3,2,1,0:T(8,128)} %apply.1, f32[2,32,128,128]{2,3,1,0:T(8,128)S(1)} %collective-permute-done.6), kind=kOutput, calls=%fused_computation.2 | convolution fusion | flops 805306368 | bytes 8454144 | tf_op jit(solution)/shard_map/dot_general | solution.py:131
  172.0 3.4 %convolution_bitcast_fusion.4 = f32[1,128,128]{2,1,0:T(8,128)S(1)} fusion(f32[2,32,128,128]{3,2,1,0:T(8,128)S(1)} %copy-done.5, f32[2,32,128,128]{3,2,1,0:T(8,128)S(1)} %copy-done), kind=kOutput, calls=%fused_computation.4 | convolution fusion | flops 805306368 | bytes 8454144 | tf_op jit(solution)/shard_map/dot_general | solution.py:131
  175.5 0.7 maximum_multiply_fusion
  176.2 27.1 %collective-permute-done.8 = f32[2,32,128,128]{2,3,1,0:T(8,128)S(1)} collective-permute-done((f32[2,32,128,128]{2,3,1,0:T(8,128)}, f32[2,32,128,128]{2,3,1,0:T(8,128)S(1)}, u32[]{:S(2)}, u32[]{:S(2)}) %collective-permute-start.8) | collective-permute-done | bytes 4194336 | tf_op jit(solution)/shard_map/ppermute | solution.py:155
  203.3 3.4 %convolution_bitcast_fusion = f32[1,128,128]{1,2,0:T(8,128)S(1)} fusion(f32[2,32,128,128]{3,2,1,0:T(8,128)S(1)} %copy-done.5, f32[2,32,128,128]{2,3,1,0:T(8,128)S(1)} %collective-permute-done.8), kind=kOutput, calls=%fused_computation | convolution fusion | flops 805306368 | bytes 8454144 | tf_op jit(solution)/shard_map/dot_general | solution.py:131
  206.7 3.4 %convolution_bitcast_fusion.1 = f32[1,128,128]{1,2,0:T(8,128)S(1)} fusion(f32[2,32,128,128]{2,3,1,0:T(8,128)S(1)} %collective-permute-done.8, f32[2,32,128,128]{3,2,1,0:T(8,128)S(1)} %copy-done), kind=kOutput, calls=%fused_computation.1 | convolution fusion | flops 805306368 | bytes 8454144 | tf_op jit(solution)/shard_map/dot_general | solution.py:131
  210.1 0.7 maximum_multiply_fusion.1
  210.8 51.6 %all-reduce.3.cloned.1.call-done = (f32[2,128,128]{1,2,0:T(8,128)}, f32[2,2,128,128]{3,2,1,0:T(8,128)}) async-done(((f32[2,128,128]{1,2,0:T(8,128)}, f32[2,2,128,128]{3,2,1,0:T(8,128)}), (f32[2,128,128]{1,2,0:T(8,128)}, f32[2,2,128,128]{3,2,1,0:T(8,128)})) %all-reduce.3.cloned.1.call-update) | async-done | bytes 393232 | tf_op jit(solution)/shard_map/psum | solution.py:181
  262.4 1.0 fusion.3
  263.5 1.3 collective-permute-start.7
  264.8 0.7 constant_dynamic-slice_fusion
  265.5 0.7 fusion.4
  273.8 4.5 %collective-permute-start.9 = (f32[2,128,128]{2,1,0:T(8,128)}, f32[2,128,128]{2,1,0:T(8,128)S(1)}, u32[]{:S(2)}, u32[]{:S(2)}) collective-permute-start(f32[2,128,128]{2,1,0:T(8,128)} %bitcast.114), channel_id=1, source_target_pairs={{3,0},{1,3},{2,1},{0,2},{7,4},{5,7},{6,5},{4,6},{11,8},{9,11},{10,... | collective-permute-start | bytes 393224 | tf_op jit(solution)/shard_map/ppermute | solution.py:184
  278.4 1.0 copy.28
  279.4 0.9 add_bitcast_fusion
  280.3 0.9 collective-permute-done.9
  281.4 0.8 slice_bitcast_fusion
  (31 shorter events, 0.6 us)
Async XLA Ops:
  7.2 16.8 %copy-start.2 = (f32[512,4,128]{2,1,0:T(4,128)S(1)}, f32[512,4,128]{2,1,0:T(4,128)}, u32[]{:S(2)}) copy-start(f32[512,4,128]{2,1,0:T(4,128)} %projector_ref.1) | copy-start | bytes 3145732
  7.2 16.8 %copy-start.3 = (s32[512]{0:T(512)S(1)}, s32[512]{0:T(512)}, u32[]{:S(2)}) copy-start(s32[512]{0:T(512)} %slot_ref.1) | copy-start | bytes 6148
  7.2 16.8 %copy-start.4 = (s32[512]{0:T(512)S(1)}, s32[512]{0:T(512)}, u32[]{:S(2)}) copy-start(s32[512]{0:T(512)} %block_ref.1) | copy-start | bytes 6148
  7.2 255.3 %all-reduce.3.cloned.1.call-start = ((), (), s32[]{:S(2)}) async-start(), calls=%async_computation | async-start | bytes 786432 | tf_op jit(solution)/shard_map/psum | solution.py:181
  12.9 114.2 %collective-permute-start.6 = (f32[2,32,128,128]{2,3,1,0:T(8,128)}, f32[2,32,128,128]{2,3,1,0:T(8,128)S(1)}, u32[]{:S(2)}, u32[]{:S(2)}) collective-permute-start(f32[2,32,128,128]{2,3,1,0:T(8,128)} %copy.19), channel_id=1, source_target_pairs={{0,1},{3,2},{4,5},{7,6},{8,9},{11,10},{12,13},{15,14},{16,17},{19,... | collective-permute-start | bytes 12582920 | tf_op jit(solution)/shard_map/ppermute | solution.py:154
  18.1 111.2 %collective-permute-start = (f32[2,32,128,128]{3,2,1,0:T(8,128)}, f32[2,32,128,128]{3,2,1,0:T(8,128)}, u32[]{:S(2)}, u32[]{:S(2)}) collective-permute-start(f32[2,32,128,128]{3,2,1,0:T(8,128)} %x_ref.1), channel_id=1, source_target_pairs={{0,4},{4,8},{8,12},{12,16},{16,20},{20,24},{24,28},{28,0},{1,5},{5... | collective-permute-start | bytes 12582920 | tf_op jit(solution)/shard_map/ppermute | solution.py:152
  18.2 111.1 %collective-permute-start.1 = (f32[2,32,128,128]{3,2,1,0:T(8,128)}, f32[2,32,128,128]{3,2,1,0:T(8,128)}, u32[]{:S(2)}, u32[]{:S(2)}) collective-permute-start(f32[2,32,128,128]{3,2,1,0:T(8,128)} %x_ref.1), channel_id=1, source_target_pairs={{4,0},{8,4},{12,8},{16,12},{20,16},{24,20},{28,24},{0,28},{5,1},{9... | collective-permute-start | bytes 12582920 | tf_op jit(solution)/shard_map/ppermute | solution.py:153
  20.8 182.4 %collective-permute-start.8 = (f32[2,32,128,128]{2,3,1,0:T(8,128)}, f32[2,32,128,128]{2,3,1,0:T(8,128)S(1)}, u32[]{:S(2)}, u32[]{:S(2)}) collective-permute-start(f32[2,32,128,128]{2,3,1,0:T(8,128)} %copy.19), channel_id=1, source_target_pairs={{0,3},{3,1},{1,2},{2,0},{4,7},{7,5},{5,6},{6,4},{8,11},{11,9},{9,1... | collective-permute-start | bytes 12582920 | tf_op jit(solution)/shard_map/ppermute | solution.py:155
  24.0 2.2 copy-start
  26.2 89.4 %copy-start.6 = (f32[64,4]{0,1:T(4,128)S(1)}, f32[64,4]{0,1:T(4,128)}, u32[]{:S(2)}) copy-start(f32[64,4]{0,1:T(4,128)} %param.11) | copy-start | bytes 3076
  67.6 45.5 %collective-permute-start.2 = (f32[4,64,128]{2,1,0:T(8,128)S(1)}, f32[4,64,128]{2,1,0:T(8,128)S(1)}, u32[]{:S(2)}, u32[]{:S(2)}) collective-permute-start(f32[4,64,128]{2,1,0:T(8,128)S(1)} %get-tuple-element.15), channel_id=1, source_target_pairs={{0,4},{4,8},{8,12},{12,16},{16,20},{20,24},{24,28},{28,0},{1,5},{5... | collective-permute-start | bytes 393224 | tf_op jit(solution)/shard_map/ppermute | solution.py:166
  113.1 2.5 collective-permute-start.3
  115.7 5.6 %collective-permute-start.5 = (f32[4,64,128]{2,1,0:T(8,128)S(1)}, f32[4,64,128]{2,1,0:T(8,128)S(1)}, u32[]{:S(2)}, u32[]{:S(2)}) collective-permute-start(f32[4,64,128]{2,1,0:T(8,128)S(1)} %fusion.2), channel_id=1, source_target_pairs={{4,0},{8,4},{12,8},{16,12},{20,16},{24,20},{28,24},{0,28},{5,1},{9... | collective-permute-start | bytes 393224 | tf_op jit(solution)/shard_map/ppermute | solution.py:171
  121.4 5.7 %collective-permute-start.4 = (f32[4,64,128]{2,1,0:T(8,128)S(1)}, f32[4,64,128]{2,1,0:T(8,128)S(1)}, u32[]{:S(2)}, u32[]{:S(2)}) collective-permute-start(f32[4,64,128]{2,1,0:T(8,128)S(1)} %fusion.2), channel_id=1, source_target_pairs={{0,4},{4,8},{8,12},{12,16},{16,20},{20,24},{24,28},{28,0},{1,5},{5... | collective-permute-start | bytes 393224 | tf_op jit(solution)/shard_map/ppermute | solution.py:171
  127.1 2.3 copy-start.1
  167.6 4.4 %copy-start.5 = (f32[2,32,128,128]{3,2,1,0:T(8,128)S(1)}, f32[2,32,128,128]{3,2,1,0:T(8,128)}, u32[]{:S(2)}) copy-start(f32[2,32,128,128]{3,2,1,0:T(8,128)} %apply.1) | copy-start | bytes 12582916
  263.5 15.9 %collective-permute-start.7 = (f32[2,128,128]{2,1,0:T(8,128)S(1)}, f32[2,128,128]{2,1,0:T(8,128)S(1)}, u32[]{:S(2)}, u32[]{:S(2)}) collective-permute-start(f32[2,128,128]{2,1,0:T(8,128)S(1)} %bitcast.116), channel_id=1, source_target_pairs={{1,0},{2,3},{5,4},{6,7},{9,8},{10,11},{13,12},{14,15},{17,16},{18,... | collective-permute-start | bytes 393224 | tf_op jit(solution)/shard_map/ppermute | solution.py:184
  273.8 7.4 %collective-permute-start.9 = (f32[2,128,128]{2,1,0:T(8,128)}, f32[2,128,128]{2,1,0:T(8,128)S(1)}, u32[]{:S(2)}, u32[]{:S(2)}) collective-permute-start(f32[2,128,128]{2,1,0:T(8,128)} %bitcast.114), channel_id=1, source_target_pairs={{3,0},{1,3},{2,1},{0,2},{7,4},{5,7},{6,5},{4,6},{11,8},{9,11},{10,... | collective-permute-start | bytes 393224 | tf_op jit(solution)/shard_map/ppermute | solution.py:184
Sparse Core Ops, SparseCore 0:
  210.9 51.4 all-reduce.2

commit v2 on v1

--- a/solution.py
+++ b/solution.py
@@ -13,8 +13,9 @@
 highest = lax.Precision.HIGHEST
 MIB = 1 << 20
 
-first_round = ((0, 3), (3, 1), (1, 2), (2, 0))
-second_round = ((0, 1), (3, 2))
+groups = 4
+next_round = tuple((i, (i + 1) % groups) for i in range(groups))
+across_round = ((0, 2), (3, 1))
 
 
 def project_kernel(slots, slot_ref, block_ref, count_ref, projector_ref, x_ref, w_ref, part_ref):
@@ -122,22 +123,177 @@
     )(orbitals, before, after, potential, scaled, weights.reshape(planes, height, depth, cells))
 
 
-def products(left, orbitals, applied):
+def gram_kernel(count, *refs):
+    *left_refs, x_ref, applied_ref, out_ref = refs
+    bf16 = jnp.bfloat16
+
+    def halves(values):
+        high = values.astype(bf16)
+        return high, (values - high.astype(jnp.float32)).astype(bf16)
+
+    def times(left, right):
+        return lax.dot_general(
+            left, right, (((0,), (0,)), ((), ())), preferred_element_type=jnp.float32
+        )
+
+    @pl.when(pl.program_id(0) == 0)
+    def _():
+        out_ref[...] = jnp.zeros_like(out_ref)
+
+    left_high, left_low = halves(jnp.concatenate([ref[...] for ref in left_refs], axis=1))
+    right_high, right_low = halves(jnp.concatenate([x_ref[...], applied_ref[...]], axis=1))
+    out_ref[...] += (
+        times(left_high, right_high) + times(left_high, right_low) + times(left_low, right_high)
+    )
+
+
+def gram(lefts, orbitals, applied):
     cols = orbitals.shape[-1]
-    left = left.reshape(-1, cols)
-    contract = (((0,), (0,)), ((), ()))
-    return jnp.stack(
-        [
-            lax.dot_general(
-                left,
-                right.reshape(-1, cols),
-                contract,
-                precision=lax.Precision.HIGH,
-                preferred_element_type=jnp.float32,
-            )
-            for right in (orbitals, applied)
-        ]
-    )
+    cells = orbitals.size // cols
+    step = min(1024, cells)
+    arrays = [x.reshape(cells, cols) for x in (*lefts, orbitals, applied)]
+    count = len(lefts)
+    out = pl.pallas_call(
+        functools.partial(gram_kernel, count),
+        grid=(cells // step,),
+        out_shape=jax.ShapeDtypeStruct((count * cols, 2 * cols), jnp.float32),
+        in_specs=[pl.BlockSpec((step, cols), lambda i: (i, 0))] * len(arrays),
+        out_specs=pl.BlockSpec((count * cols, 2 * cols), lambda i: (0, 0)),
+        compiler_params=pltpu.CompilerParams(vmem_limit_bytes=32 * MIB),
+        cost_estimate=pl.CostEstimate(
+            flops=12 * count * cells * cols * cols,
+            bytes_accessed=4 * (count + 2) * cells * cols,
+            transcendentals=0,
+        ),
+        name="gram",
+    )(*arrays)
+    return jnp.swapaxes(out.reshape(count, cols, 2, cols), 1, 2)
+
+
+def reduce_kernel(
+    slabs, part_ref, overlap_ref, operator_ref,
+    landed, summed, mirrored, gathered, send_one, recv_one, send_two, recv_two, send_three, recv_three,
+):
+    slab = lax.axis_index("slab")
+    band = lax.axis_index("band")
+    here_next = lax.rem(band + 1, groups)
+    here_previous = lax.rem(band + groups - 1, groups)
+    here_across = lax.rem(band + 2, groups)
+    cols = overlap_ref.shape[1]
+    mesh_type = pl.DeviceIdType.MESH
+
+    barrier = pltpu.get_barrier_semaphore()
+
+    @pl.loop(1, slabs)
+    def _(d):
+        pl.semaphore_signal(
+            barrier, inc=1, device_id=(lax.rem(slab + d, slabs), band), device_id_type=mesh_type
+        )
+
+    for other in (here_next, here_previous, here_across):
+        pl.semaphore_signal(barrier, inc=1, device_id=(slab, other), device_id_type=mesh_type)
+    pl.semaphore_wait(barrier, slabs - 1 + 3)
+
+    def scatter(d):
+        peer = lax.rem(slab + d, slabs)
+        return pltpu.make_async_remote_copy(
+            src_ref=part_ref.at[peer],
+            dst_ref=landed.at[d - 1],
+            send_sem=send_one.at[d - 1],
+            recv_sem=recv_one.at[d - 1],
+            device_id=(peer, band),
+            device_id_type=mesh_type,
+        )
+
+    @pl.loop(1, slabs)
+    def _(d):
+        scatter(d).start()
+
+    summed[...] = part_ref[slab]
+
+    @pl.loop(1, slabs)
+    def _(d):
+        scatter(d).wait()
+        summed[...] += landed[d - 1]
+
+    exchanges = [
+        pltpu.make_async_remote_copy(
+            src_ref=summed.at[block],
+            dst_ref=mirrored.at[place],
+            send_sem=send_two.at[place],
+            recv_sem=recv_two.at[place],
+            device_id=(slab, other),
+            device_id_type=mesh_type,
+        )
+        for place, (block, other) in enumerate(((1, here_across), (2, here_previous)))
+    ]
+    for exchange in exchanges:
+        exchange.start()
+    for exchange in exchanges:
+        exchange.wait()
+
+    gave = (band == across_round[0][0]) | (band == across_round[1][0])
+    gathered[slab, 0] = summed[0]
+    gathered[slab, 1] = jnp.where(gave, mirrored[0], summed[1])
+    gathered[slab, 2] = summed[2]
+    gathered[slab, 3] = mirrored[1]
+
+    def spread(d):
+        return pltpu.make_async_remote_copy(
+            src_ref=gathered.at[slab],
+            dst_ref=gathered.at[slab],
+            send_sem=send_three.at[d - 1],
+            recv_sem=recv_three.at[d - 1],
+            device_id=(lax.rem(slab + d, slabs), band),
+            device_id_type=mesh_type,
+        )
+
+    @pl.loop(1, slabs)
+    def _(d):
+        spread(d).start()
+
+    @pl.loop(1, slabs)
+    def _(d):
+        spread(d).wait()
+
+    for block, other in enumerate((band, here_across, here_previous, here_next)):
+        values = gathered[:, block].reshape(2, cols, cols)
+        rows = pl.ds(pl.multiple_of(other * cols, cols), cols)
+        for ref, value in ((overlap_ref, values[0]), (operator_ref, values[1])):
+            if block == 1:
+                value = jnp.where(gave, value.T, value)
+            if block == 3:
+                value = value.T
+            ref[rows, :] = value
+
+
+def reduce(parts, slabs):
+    blocks, _, cols, _ = parts.shape
+    rows = 2 * cols // slabs
+    parts = jnp.swapaxes(parts.reshape(blocks, slabs, rows, cols), 0, 1)
+    vmem = pl.BlockSpec(memory_space=pltpu.VMEM)
+    return pl.pallas_call(
+        functools.partial(reduce_kernel, slabs),
+        out_shape=(jax.ShapeDtypeStruct((groups * cols, cols), jnp.float32),) * 2,
+        in_specs=[vmem],
+        out_specs=(vmem, vmem),
+        scratch_shapes=[
+            pltpu.VMEM((slabs - 1, blocks, rows, cols), jnp.float32),
+            pltpu.VMEM((blocks, rows, cols), jnp.float32),
+            pltpu.VMEM((2, rows, cols), jnp.float32),
+            pltpu.VMEM((slabs, groups, rows, cols), jnp.float32),
+            pltpu.SemaphoreType.DMA((slabs - 1,)),
+            pltpu.SemaphoreType.DMA((slabs - 1,)),
+            pltpu.SemaphoreType.DMA((2,)),
+            pltpu.SemaphoreType.DMA((2,)),
+            pltpu.SemaphoreType.DMA((slabs - 1,)),
+            pltpu.SemaphoreType.DMA((slabs - 1,)),
+        ],
+        compiler_params=pltpu.CompilerParams(
+            collective_id=0, has_side_effects=True, vmem_limit_bytes=32 * MIB
+        ),
+        name="reduce",
+    )(parts)
 
 
 def local(orbitals, potential, projector, strength, entry_slot, entry_block, entry_count):
@@ -147,12 +303,11 @@
     slabs = lax.axis_size("slab")
     up = [(i, (i + 1) % slabs) for i in range(slabs)]
     down = [(j, i) for i, j in up]
-    band = lax.axis_index("band")
 
     before = lax.ppermute(orbitals, "slab", up)
     after = lax.ppermute(orbitals, "slab", down)
-    met_second = lax.ppermute(orbitals, "band", second_round)
-    met_first = lax.ppermute(orbitals, "band", first_round)
+    met_across = lax.ppermute(orbitals, "band", across_round)
+    met_next = lax.ppermute(orbitals, "band", next_round)
 
     weights, partial_value = project(
         entry_slot,
@@ -174,31 +329,10 @@
     applied = apply(orbitals, before, after, potential, beside_all, weights)
 
     volume = 1.0 / (slabs * planes * height * cells)
-    early = jnp.stack(
-        [products(orbitals, orbitals, applied), products(met_second, orbitals, applied)]
-    )
-    own, second = lax.psum(early * volume, "slab")
-    first = lax.psum(products(met_first, orbitals, applied) * volume, "slab")
-
-    def mirror(blocks, pairs):
-        return lax.ppermute(
-            jnp.swapaxes(blocks, 1, 2), "band", [(there, here) for here, there in pairs]
-        )
-
-    second = second + mirror(second, second_round)
-    mirrored = mirror(first, first_round)
-    found = jnp.stack([own, second, first, mirrored])
-    kinds = [[0] * 4 for _ in range(4)]
-    for here, there in second_round:
-        kinds[here][there] = kinds[there][here] = 1
-    for here, there in first_round:
-        kinds[there][here] = 2
-        kinds[here][there] = 3
-    order = jnp.array(kinds, jnp.int32)[band]
-    rows = jnp.concatenate(
-        [lax.dynamic_index_in_dim(found, order[r], 0, keepdims=False) for r in range(4)], axis=1
-    )
-    return applied, rows[0], rows[1]
+    early = gram((orbitals, met_across), orbitals, applied)
+    late = gram((met_next,), orbitals, applied)
+    correlation, subspace = reduce(jnp.concatenate([early, late]) * volume, slabs)
+    return applied, correlation, subspace
 
 
 def solution(mesh):

time: 290 us -> 221 us (0.76)
  waiting for transfers between devices: 132 us -> 79.8 us
  Pallas kernels: 79.7 us -> 110 us
  between operations: 22.6 us -> 1.42 us
  matrix products: 20.3 us -> 0 us
  starting transfers between devices: 19.7 us -> 16.1 us
    psum x1 -> x0, waiting for transfers between devices: 51.6 us -> none  [local(): first = lax.psum(products(met_first, orbitals, applied) * volume, 'slab')]
    pallas_call x0 -> x3, Pallas kernels: none -> 29.6 us  [the longest x1 17.4 us: reduce(): pl.pallas_call(functools.partial(reduce_kernel, slabs), out_shape=(jax.Sh...]
    dot_general x6 -> x0, matrix products: 20.3 us -> none  [products(): lax.dot_general(left, right.reshape(-1, cols), contract, precision=lax.Pr...]
    ppermute x1, waiting for transfers between devices: 45.4 us -> 37 us  [local(): from_left = lax.ppermute(partial_value[:, 2], 'slab', up)]
    ppermute x4 -> x2, starting transfers between devices: 13.5 us -> 5.51 us  [the longest x1 5.44 us: local(): met_across = lax.ppermute(orbitals, 'band', across_round)]
    ppermute x4 -> x2, waiting for transfers between devices: 27.9 us -> 34.3 us  [the longest x1 34.3 us: local(): met_next = lax.ppermute(orbitals, 'band', next_round)]
    unnamed x15 -> x22, local copies, waits for them, and re-layouts: 7.92 us -> 12.7 us
  transfers between devices with their start and end apart: 11 -> 8, of which waited for: 7 -> 5; matrix products, arithmetic and copies ran while one was open for 6% -> 0% of each run, Pallas kernels for 28% -> 39%
where the time goes in v2:
time: 221 us; the launch traced here: 220 us
  Pallas kernels  110 us (50%)
  waiting for transfers between devices  79.8 us (36%)
  starting transfers between devices  16.1 us (7%)
  local copies, waits for them, and re-layouts  13 us (6%)
    pallas_call x1, Pallas kernels, project(): pl.pallas_call(functools.partial(project_kernel, slots), out_shape=(jax.S...  41.5 us
    pallas_call x1, Pallas kernels, apply(): pl.pallas_call(apply_kernel, grid=(height,), out_shape=jax.ShapeDtypeStru...  38.5 us
    ppermute x1, waiting for transfers between devices, local(): from_left = lax.ppermute(partial_value[:, 2], 'slab', up)  37 us
    ppermute x1, waiting for transfers between devices, local(): met_next = lax.ppermute(orbitals, 'band', next_round)  34.3 us
    pallas_call x1, Pallas kernels, reduce(): pl.pallas_call(functools.partial(reduce_kernel, slabs), out_shape=(jax.Sh...  17.4 us
    unnamed x22, local copies, waits for them, and re-layouts  12.7 us
    pallas_call x2, Pallas kernels, gram(): pl.pallas_call(functools.partial(gram_kernel, count), grid=(cells // step...  12.2 us
    ppermute x1, starting transfers between devices, local(): met_across = lax.ppermute(orbitals, 'band', across_round)  5.44 us
  transfers between devices with their start and end apart: 8, of which 5 were waited for; matrix products, arithmetic and copies ran while one was open for 0% of the time, Pallas kernels for 39%

profile of v2, /device:TPU:0, one launch (start us, length us, event | category | flops | bytes accessed | tf_op | source)
XLA Modules:
  0.0 220.0 jit_solution(1116705606302226103)
XLA Ops:
  0.6 0.5 collective-permute-start
  1.1 2.9 %collective-permute-start.1 = (f32[2,32,128,128]{3,2,1,0:T(8,128)}, f32[2,32,128,128]{3,2,1,0:T(8,128)}, u32[]{:S(2)}, u32[]{:S(2)}) collective-permute-start(f32[2,32,128,128]{3,2,1,0:T(8,128)} %x_ref.1), channel_id=1, source_target_pairs={{4,0},{8,4},{12,8},{16,12},{20,16},{24,20},{28,24},{0,28},{5,1},{9... | collective-permute-start | bytes 12582920 | tf_op jit(solution)/shard_map/ppermute | solution.py:308
  4.1 5.4 %collective-permute-start.6 = (f32[2,32,128,128]{3,2,1,0:T(8,128)}, f32[2,32,128,128]{3,2,1,0:T(8,128)S(1)}, u32[]{:S(2)}, u32[]{:S(2)}) collective-permute-start(f32[2,32,128,128]{3,2,1,0:T(8,128)} %x_ref.1), channel_id=1, source_target_pairs={{0,2},{3,1},{4,6},{7,5},{8,10},{11,9},{12,14},{15,13},{16,18},{19,... | collective-permute-start | bytes 12582920 | tf_op jit(solution)/shard_map/ppermute | solution.py:309
  9.5 0.1 collective-permute-start.7
  10.3 2.2 copy-done
  12.4 1.2 copy-done.6
  13.7 0.7 copy-done.7
  14.4 0.7 copy-done.8
  15.0 41.5 %project.1 = (f32[64,768,128]{2,1,0:T(8,128)}, f32[768,128]{1,0:T(8,128)S(1)}) custom-call(s32[512]{0:T(512)S(1)} %copy-done.7, s32[512]{0:T(512)S(1)} %copy-done.8, s32[1]{0:T(128)S(6)} %copy.31.count_ref, f32[512,4,128]{2,1,0:T(4,128)S(1)} %copy-done.6, f32[64,128,128]{2,1,0:T(8,128)S(1)} %bitcast.42), custom_call_target="tpu_custom_call" | custom-call | flops 9663676416 | bytes 25165824 | tf_op jit(solution)/shard_map/project/pallas_call | solution.py:53
  56.6 2.0 collective-permute-start.2
  58.5 37.0 %collective-permute-done.2 = f32[4,64,128]{2,1,0:T(8,128)S(1)} collective-permute-done((f32[4,64,128]{2,1,0:T(8,128)S(1)}, f32[4,64,128]{2,1,0:T(8,128)S(1)}, u32[]{:S(2)}, u32[]{:S(2)}) %collective-permute-start.2) | collective-permute-done | bytes 131104 | tf_op jit(solution)/shard_map/ppermute | solution.py:321
  95.5 0.0 collective-permute-start.3
  95.5 2.5 %collective-permute-done.3 = f32[4,64,128]{2,1,0:T(8,128)S(1)} collective-permute-done((f32[4,64,128]{2,1,0:T(8,128)S(1)}, f32[4,64,128]{2,1,0:T(8,128)S(1)}, u32[]{:S(2)}, u32[]{:S(2)}) %collective-permute-start.3) | collective-permute-done | bytes 131104 | tf_op jit(solution)/shard_map/ppermute | solution.py:322
  98.0 0.1 fusion.3
  98.1 2.8 %collective-permute-start.5 = (f32[4,64,128]{2,1,0:T(8,128)S(1)}, f32[4,64,128]{2,1,0:T(8,128)S(1)}, u32[]{:S(2)}, u32[]{:S(2)}) collective-permute-start(f32[4,64,128]{2,1,0:T(8,128)S(1)} %fusion.3), channel_id=1, source_target_pairs={{4,0},{8,4},{12,8},{16,12},{20,16},{24,20},{28,24},{0,28},{5,1},{9... | collective-permute-start | bytes 393224 | tf_op jit(solution)/shard_map/ppermute | solution.py:326
  101.0 2.5 %collective-permute-done.5 = f32[4,64,128]{2,1,0:T(8,128)S(1)} collective-permute-done((f32[4,64,128]{2,1,0:T(8,128)S(1)}, f32[4,64,128]{2,1,0:T(8,128)S(1)}, u32[]{:S(2)}, u32[]{:S(2)}) %collective-permute-start.5) | collective-permute-done | bytes 131104 | tf_op jit(solution)/shard_map/ppermute | solution.py:326
  103.5 2.3 %collective-permute-start.4 = (f32[4,64,128]{2,1,0:T(8,128)S(1)}, f32[4,64,128]{2,1,0:T(8,128)S(1)}, u32[]{:S(2)}, u32[]{:S(2)}) collective-permute-start(f32[4,64,128]{2,1,0:T(8,128)S(1)} %fusion.3), channel_id=1, source_target_pairs={{0,4},{4,8},{8,12},{12,16},{16,20},{20,24},{24,28},{28,0},{1,5},{5... | collective-permute-start | bytes 393224 | tf_op jit(solution)/shard_map/ppermute | solution.py:326
  105.8 3.5 %collective-permute-done.4 = f32[4,64,128]{2,1,0:T(8,128)S(1)} collective-permute-done((f32[4,64,128]{2,1,0:T(8,128)S(1)}, f32[4,64,128]{2,1,0:T(8,128)S(1)}, u32[]{:S(2)}, u32[]{:S(2)}) %collective-permute-start.4) | collective-permute-done | bytes 131104 | tf_op jit(solution)/shard_map/ppermute | solution.py:326
  109.3 0.0 collective-permute-done.before_ref
  109.4 0.0 collective-permute-done.1.after_ref
  109.4 38.5 %apply.1 = f32[2,32,128,128]{3,2,1,0:T(8,128)} custom-call(f32[2,32,128,128]{3,2,1,0:T(8,128)S(1)} %copy-done.1, f32[2,32,128,128]{3,2,1,0:T(8,128)} %collective-permute-done.before_ref, f32[2,32,128,128]{3,2,1,0:T(8,128)} %collective-permute-done.1.after_ref, f32[2,32,128]{2,1,0:T(8,128)S(1)} %copy-done.5, f32[768,128]{1,0:T(8,128)S(1)} %bitcast.49, ...), custom_call_target="tpu_custom_call" | custom-call | flops 9663676416 | bytes 25165824 | tf_op jit(solution)/shard_map/apply/pallas_call | solution.py:110
  147.9 2.2 copy-done.3
  150.1 5.7 %gram.2 = f32[256,256]{1,0:T(8,128)S(1)} custom-call(f32[8192,128]{1,0:T(8,128)S(1)} %bitcast.43, f32[8192,128]{1,0:T(8,128)S(1)} %bitcast.48, f32[8192,128]{1,0:T(8,128)S(1)} %bitcast.44, f32[8192,128]{1,0:T(8,128)S(1)} %bitcast.46), custom_call_target="tpu_custom_call" | custom-call | flops 3221225472 | bytes 16777216 | tf_op jit(solution)/shard_map/gram/pallas_call | solution.py:156
  155.8 0.1 reshape.50
  156.0 34.3 %collective-permute-done.7 = f32[2,32,128,128]{3,2,1,0:T(8,128)} collective-permute-done((f32[2,32,128,128]{3,2,1,0:T(8,128)}, f32[2,32,128,128]{3,2,1,0:T(8,128)}, u32[]{:S(2)}, u32[]{:S(2)}) %collective-permute-start.7) | collective-permute-done | bytes 4194336 | tf_op jit(solution)/shard_map/ppermute | solution.py:310
  190.2 2.2 copy-done.2
  192.4 2.2 copy-done.4
  194.6 6.5 %gram.3 = f32[128,256]{1,0:T(8,128)S(1)} custom-call(f32[8192,128]{1,0:T(8,128)} %bitcast.18.refs_0_, f32[8192,128]{1,0:T(8,128)S(1)} %bitcast.45, f32[8192,128]{1,0:T(8,128)S(1)} %bitcast.47), custom_call_target="tpu_custom_call" | custom-call | flops 1610612736 | bytes 12582912 | tf_op jit(solution)/shard_map/gram/pallas_call | solution.py:156
  201.1 0.1 reshape.52
  201.2 17.4 %reduce.1 = (f32[512,128]{1,0:T(8,128)S(1)}, f32[512,128]{1,0:T(8,128)S(1)}) custom-call(f32[8,3,32,128]{3,2,1,0:T(8,128)S(1)} %fusion.part_ref), custom_call_target="tpu_custom_call" | custom-call | tf_op jit(solution)/shard_map/reduce/pallas_call | solution.py:275
  218.6 0.7 copy.32
  219.3 0.7 copy.33
  (19 shorter events, 0.1 us)
Async XLA Ops:
  0.6 108.7 %collective-permute-start = (f32[2,32,128,128]{3,2,1,0:T(8,128)}, f32[2,32,128,128]{3,2,1,0:T(8,128)}, u32[]{:S(2)}, u32[]{:S(2)}) collective-permute-start(f32[2,32,128,128]{3,2,1,0:T(8,128)} %x_ref.1), channel_id=1, source_target_pairs={{0,4},{4,8},{8,12},{12,16},{16,20},{20,24},{24,28},{28,0},{1,5},{5... | collective-permute-start | bytes 12582920 | tf_op jit(solution)/shard_map/ppermute | solution.py:307
  1.1 108.2 %collective-permute-start.1 = (f32[2,32,128,128]{3,2,1,0:T(8,128)}, f32[2,32,128,128]{3,2,1,0:T(8,128)}, u32[]{:S(2)}, u32[]{:S(2)}) collective-permute-start(f32[2,32,128,128]{3,2,1,0:T(8,128)} %x_ref.1), channel_id=1, source_target_pairs={{4,0},{8,4},{12,8},{16,12},{20,16},{24,20},{28,24},{0,28},{5,1},{9... | collective-permute-start | bytes 12582920 | tf_op jit(solution)/shard_map/ppermute | solution.py:308
  4.1 143.8 %collective-permute-start.6 = (f32[2,32,128,128]{3,2,1,0:T(8,128)}, f32[2,32,128,128]{3,2,1,0:T(8,128)S(1)}, u32[]{:S(2)}, u32[]{:S(2)}) collective-permute-start(f32[2,32,128,128]{3,2,1,0:T(8,128)} %x_ref.1), channel_id=1, source_target_pairs={{0,2},{3,1},{4,6},{7,5},{8,10},{11,9},{12,14},{15,13},{16,18},{19,... | collective-permute-start | bytes 12582920 | tf_op jit(solution)/shard_map/ppermute | solution.py:309
  9.5 180.7 %collective-permute-start.7 = (f32[2,32,128,128]{3,2,1,0:T(8,128)}, f32[2,32,128,128]{3,2,1,0:T(8,128)}, u32[]{:S(2)}, u32[]{:S(2)}) collective-permute-start(f32[2,32,128,128]{3,2,1,0:T(8,128)} %x_ref.1), channel_id=1, source_target_pairs={{0,1},{1,2},{2,3},{3,0},{4,5},{5,6},{6,7},{7,4},{8,9},{9,10},{10,1... | collective-permute-start | bytes 12582920 | tf_op jit(solution)/shard_map/ppermute | solution.py:310
  10.3 2.2 copy-start
  12.4 1.2 copy-start.6
  13.7 0.7 copy-start.7
  14.3 0.7 copy-start.8
  15.0 83.0 %copy-start.9 = (f32[64,4]{0,1:T(4,128)S(1)}, f32[64,4]{0,1:T(4,128)}, u32[]{:S(2)}) copy-start(f32[64,4]{0,1:T(4,128)} %param.10) | copy-start | bytes 3076
  15.0 94.3 %copy-start.1 = (f32[2,32,128,128]{3,2,1,0:T(8,128)S(1)}, f32[2,32,128,128]{3,2,1,0:T(8,128)}, u32[]{:S(2)}) copy-start(f32[2,32,128,128]{3,2,1,0:T(8,128)} %x_ref.1) | copy-start | bytes 12582916
  15.0 94.3 %copy-start.5 = (f32[2,32,128]{2,1,0:T(8,128)S(1)}, f32[2,32,128]{2,1,0:T(8,128)}, u32[]{:S(2)}) copy-start(f32[2,32,128]{2,1,0:T(8,128)} %potential_ref.1) | copy-start | bytes 98308
  56.6 39.0 %collective-permute-start.2 = (f32[4,64,128]{2,1,0:T(8,128)S(1)}, f32[4,64,128]{2,1,0:T(8,128)S(1)}, u32[]{:S(2)}, u32[]{:S(2)}) collective-permute-start(f32[4,64,128]{2,1,0:T(8,128)S(1)} %get-tuple-element.11), channel_id=1, source_target_pairs={{0,4},{4,8},{8,12},{12,16},{16,20},{20,24},{24,28},{28,0},{1,5},{5... | collective-permute-start | bytes 393224 | tf_op jit(solution)/shard_map/ppermute | solution.py:321
  95.5 2.5 %collective-permute-start.3 = (f32[4,64,128]{2,1,0:T(8,128)S(1)}, f32[4,64,128]{2,1,0:T(8,128)S(1)}, u32[]{:S(2)}, u32[]{:S(2)}) collective-permute-start(f32[4,64,128]{2,1,0:T(8,128)S(1)} %get-tuple-element.12), channel_id=1, source_target_pairs={{4,0},{8,4},{12,8},{16,12},{20,16},{24,20},{28,24},{0,28},{5,1},{9... | collective-permute-start | bytes 393224 | tf_op jit(solution)/shard_map/ppermute | solution.py:322
  98.1 5.3 %collective-permute-start.5 = (f32[4,64,128]{2,1,0:T(8,128)S(1)}, f32[4,64,128]{2,1,0:T(8,128)S(1)}, u32[]{:S(2)}, u32[]{:S(2)}) collective-permute-start(f32[4,64,128]{2,1,0:T(8,128)S(1)} %fusion.3), channel_id=1, source_target_pairs={{4,0},{8,4},{12,8},{16,12},{20,16},{24,20},{28,24},{0,28},{5,1},{9... | collective-permute-start | bytes 393224 | tf_op jit(solution)/shard_map/ppermute | solution.py:326
  103.5 5.8 %collective-permute-start.4 = (f32[4,64,128]{2,1,0:T(8,128)S(1)}, f32[4,64,128]{2,1,0:T(8,128)S(1)}, u32[]{:S(2)}, u32[]{:S(2)}) collective-permute-start(f32[4,64,128]{2,1,0:T(8,128)S(1)} %fusion.3), channel_id=1, source_target_pairs={{0,4},{4,8},{8,12},{12,16},{16,20},{20,24},{24,28},{28,0},{1,5},{5... | collective-permute-start | bytes 393224 | tf_op jit(solution)/shard_map/ppermute | solution.py:326
  147.9 2.2 copy-start.3
  190.2 2.2 copy-start.2
  192.4 2.2 copy-start.4

commit v3 on v2

--- a/solution.py
+++ b/solution.py
@@ -159,7 +159,7 @@
         out_shape=jax.ShapeDtypeStruct((count * cols, 2 * cols), jnp.float32),
         in_specs=[pl.BlockSpec((step, cols), lambda i: (i, 0))] * len(arrays),
         out_specs=pl.BlockSpec((count * cols, 2 * cols), lambda i: (0, 0)),
-        compiler_params=pltpu.CompilerParams(vmem_limit_bytes=32 * MIB),
+        compiler_params=pltpu.CompilerParams(vmem_limit_bytes=60 * MIB),
         cost_estimate=pl.CostEstimate(
             flops=12 * count * cells * cols * cols,
             bytes_accessed=4 * (count + 2) * cells * cols,
@@ -170,9 +170,88 @@
     return jnp.swapaxes(out.reshape(count, cols, 2, cols), 1, 2)
 
 
-def reduce_kernel(
-    slabs, part_ref, overlap_ref, operator_ref,
-    landed, summed, mirrored, gathered, send_one, recv_one, send_two, recv_two, send_three, recv_three,
+mesh_type = pl.DeviceIdType.MESH
+
+
+def greet(slabs, others):
+    slab = lax.axis_index("slab")
+    band = lax.axis_index("band")
+    barrier = pltpu.get_barrier_semaphore()
+
+    @pl.loop(1, slabs)
+    def _(d):
+        pl.semaphore_signal(
+            barrier, inc=1, device_id=(lax.rem(slab + d, slabs), band), device_id_type=mesh_type
+        )
+
+    for other in others:
+        pl.semaphore_signal(barrier, inc=1, device_id=(slab, other), device_id_type=mesh_type)
+    pl.semaphore_wait(barrier, slabs - 1 + len(others))
+
+
+def slab_sum(slabs, part_ref, landed, summed, sends, recvs):
+    slab = lax.axis_index("slab")
+    band = lax.axis_index("band")
+
+    def scatter(d):
+        peer = lax.rem(slab + d, slabs)
+        return pltpu.make_async_remote_copy(
+            src_ref=part_ref.at[peer],
+            dst_ref=landed.at[d - 1],
+            send_sem=sends.at[d - 1],
+            recv_sem=recvs.at[d - 1],
+            device_id=(peer, band),
+            device_id_type=mesh_type,
+        )
+
+    @pl.loop(1, slabs)
+    def _(d):
+        scatter(d).start()
+
+    summed[...] = part_ref[slab]
+
+    @pl.loop(1, slabs)
+    def _(d):
+        scatter(d).wait()
+        summed[...] += landed[d - 1]
+
+
+def slab_spread(slabs, gathered, sends, recvs):
+    slab = lax.axis_index("slab")
+    band = lax.axis_index("band")
+
+    def spread(d):
+        return pltpu.make_async_remote_copy(
+            src_ref=gathered.at[slab],
+            dst_ref=gathered.at[slab],
+            send_sem=sends.at[d - 1],
+            recv_sem=recvs.at[d - 1],
+            device_id=(lax.rem(slab + d, slabs), band),
+            device_id_type=mesh_type,
+        )
+
+    @pl.loop(1, slabs)
+    def _(d):
+        spread(d).start()
+
+    @pl.loop(1, slabs)
+    def _(d):
+        spread(d).wait()
+
+
+def early_kernel(slabs, part_ref, out_ref, landed, summed, gathered, *sems):
+    send_one, recv_one, send_two, recv_two = sems
+    greet(slabs, ())
+    slab_sum(slabs, part_ref, landed, summed, send_one, recv_one)
+    gathered[lax.axis_index("slab")] = summed[...]
+    slab_spread(slabs, gathered, send_two, recv_two)
+    for block in range(out_ref.shape[0]):
+        out_ref[block] = gathered[:, block].reshape(out_ref.shape[1:])
+
+
+def late_kernel(
+    slabs, part_ref, early_ref, overlap_ref, operator_ref,
+    landed, summed, mirrored, gathered, crossed, send_one, recv_one, send_two, recv_two, send_three, recv_three,
 ):
     slab = lax.axis_index("slab")
     band = lax.axis_index("band")
@@ -180,108 +259,86 @@
     here_previous = lax.rem(band + groups - 1, groups)
     here_across = lax.rem(band + 2, groups)
     cols = overlap_ref.shape[1]
-    mesh_type = pl.DeviceIdType.MESH
-
-    barrier = pltpu.get_barrier_semaphore()
-
-    @pl.loop(1, slabs)
-    def _(d):
-        pl.semaphore_signal(
-            barrier, inc=1, device_id=(lax.rem(slab + d, slabs), band), device_id_type=mesh_type
-        )
-
-    for other in (here_next, here_previous, here_across):
-        pl.semaphore_signal(barrier, inc=1, device_id=(slab, other), device_id_type=mesh_type)
-    pl.semaphore_wait(barrier, slabs - 1 + 3)
-
-    def scatter(d):
-        peer = lax.rem(slab + d, slabs)
+
+    greet(slabs, (here_next, here_previous, here_across))
+
+    def exchange(source, target, place, other):
         return pltpu.make_async_remote_copy(
-            src_ref=part_ref.at[peer],
-            dst_ref=landed.at[d - 1],
-            send_sem=send_one.at[d - 1],
-            recv_sem=recv_one.at[d - 1],
-            device_id=(peer, band),
-            device_id_type=mesh_type,
-        )
-
-    @pl.loop(1, slabs)
-    def _(d):
-        scatter(d).start()
-
-    summed[...] = part_ref[slab]
-
-    @pl.loop(1, slabs)
-    def _(d):
-        scatter(d).wait()
-        summed[...] += landed[d - 1]
-
-    exchanges = [
-        pltpu.make_async_remote_copy(
-            src_ref=summed.at[block],
-            dst_ref=mirrored.at[place],
+            src_ref=source,
+            dst_ref=target,
             send_sem=send_two.at[place],
             recv_sem=recv_two.at[place],
             device_id=(slab, other),
             device_id_type=mesh_type,
         )
-        for place, (block, other) in enumerate(((1, here_across), (2, here_previous)))
-    ]
-    for exchange in exchanges:
-        exchange.start()
-    for exchange in exchanges:
-        exchange.wait()
+
+    crossing = exchange(early_ref.at[1], crossed, 0, here_across)
+    crossing.start()
+    slab_sum(slabs, part_ref, landed, summed, send_one, recv_one)
+    mirror = exchange(summed.at[0], mirrored, 1, here_previous)
+    mirror.start()
+    mirror.wait()
+    gathered[slab, 0] = summed[0]
+    gathered[slab, 1] = mirrored[...]
+    slab_spread(slabs, gathered, send_three, recv_three)
+    crossing.wait()
+
+    def place_rows(other, which):
+        rows = pl.ds(pl.multiple_of(other * cols, cols), cols)
+        for i, ref in enumerate((overlap_ref, operator_ref)):
+            ref[rows, :] = which(i)
 
     gave = (band == across_round[0][0]) | (band == across_round[1][0])
-    gathered[slab, 0] = summed[0]
-    gathered[slab, 1] = jnp.where(gave, mirrored[0], summed[1])
-    gathered[slab, 2] = summed[2]
-    gathered[slab, 3] = mirrored[1]
-
-    def spread(d):
-        return pltpu.make_async_remote_copy(
-            src_ref=gathered.at[slab],
-            dst_ref=gathered.at[slab],
-            send_sem=send_three.at[d - 1],
-            recv_sem=recv_three.at[d - 1],
-            device_id=(lax.rem(slab + d, slabs), band),
-            device_id_type=mesh_type,
-        )
-
-    @pl.loop(1, slabs)
-    def _(d):
-        spread(d).start()
-
-    @pl.loop(1, slabs)
-    def _(d):
-        spread(d).wait()
-
-    for block, other in enumerate((band, here_across, here_previous, here_next)):
-        values = gathered[:, block].reshape(2, cols, cols)
-        rows = pl.ds(pl.multiple_of(other * cols, cols), cols)
-        for ref, value in ((overlap_ref, values[0]), (operator_ref, values[1])):
-            if block == 1:
-                value = jnp.where(gave, value.T, value)
-            if block == 3:
-                value = value.T
-            ref[rows, :] = value
-
-
-def reduce(parts, slabs):
+    met = gathered[:, 0].reshape(2, cols, cols)
+    back = gathered[:, 1].reshape(2, cols, cols)
+    place_rows(band, lambda i: early_ref[0, i])
+    place_rows(here_across, lambda i: jnp.where(gave, crossed[i].T, early_ref[1, i]))
+    place_rows(here_previous, lambda i: met[i])
+    place_rows(here_next, lambda i: back[i].T)
+
+
+def pieces(parts, slabs):
+    blocks, _, cols, _ = parts.shape
+    return jnp.swapaxes(parts.reshape(blocks, slabs, 2 * cols // slabs, cols), 0, 1)
+
+
+def early_reduce(parts, slabs):
     blocks, _, cols, _ = parts.shape
     rows = 2 * cols // slabs
-    parts = jnp.swapaxes(parts.reshape(blocks, slabs, rows, cols), 0, 1)
     vmem = pl.BlockSpec(memory_space=pltpu.VMEM)
     return pl.pallas_call(
-        functools.partial(reduce_kernel, slabs),
+        functools.partial(early_kernel, slabs),
+        out_shape=jax.ShapeDtypeStruct(parts.shape, jnp.float32),
+        in_specs=[vmem],
+        out_specs=vmem,
+        scratch_shapes=[
+            pltpu.VMEM((slabs - 1, blocks, rows, cols), jnp.float32),
+            pltpu.VMEM((blocks, rows, cols), jnp.float32),
+            pltpu.VMEM((slabs, blocks, rows, cols), jnp.float32),
+        ]
+        + [pltpu.SemaphoreType.DMA((slabs - 1,))] * 4,
+        compiler_params=pltpu.CompilerParams(
+            collective_id=0, has_side_effects=True, vmem_limit_bytes=32 * MIB
+        ),
+        name="early_reduce",
+    )(pieces(parts, slabs))
+
+
+def late_reduce(parts, early, slabs):
+    blocks, _, cols, _ = parts.shape
+    rows = 2 * cols // slabs
+    vmem = pl.BlockSpec(memory_space=pltpu.VMEM)
+    return pl.pallas_call(
+        functools.partial(late_kernel, slabs),
         out_shape=(jax.ShapeDtypeStruct((groups * cols, cols), jnp.float32),) * 2,
-        in_specs=[vmem],
+        in_specs=[vmem, vmem],
         out_specs=(vmem, vmem),
         scratch_shapes=[
             pltpu.VMEM((slabs - 1, blocks, rows, cols), jnp.float32),
             pltpu.VMEM((blocks, rows, cols), jnp.float32),
-            pltpu.VMEM((2, rows, cols), jnp.float32),
-            pltpu.VMEM((slabs, groups, rows, cols), jnp.float32),
+            pltpu.VMEM((rows, cols), jnp.float32),
+            pltpu.VMEM((slabs, 2, rows, cols), jnp.float32),
+            pltpu.VMEM((2, cols, cols), jnp.float32),
             pltpu.SemaphoreType.DMA((slabs - 1,)),
             pltpu.SemaphoreType.DMA((slabs - 1,)),
             pltpu.SemaphoreType.DMA((2,)),
@@ -290,10 +347,10 @@
             pltpu.SemaphoreType.DMA((slabs - 1,)),
         ],
         compiler_params=pltpu.CompilerParams(
-            collective_id=0, has_side_effects=True, vmem_limit_bytes=32 * MIB
-        ),
-        name="reduce",
-    )(parts)
+            collective_id=1, has_side_effects=True, vmem_limit_bytes=32 * MIB
+        ),
+        name="late_reduce",
+    )(pieces(parts, slabs), early)
 
 
 def local(orbitals, potential, projector, strength, entry_slot, entry_block, entry_count):
@@ -304,10 +361,10 @@
     up = [(i, (i + 1) % slabs) for i in range(slabs)]
     down = [(j, i) for i, j in up]
 
+    met_across = lax.ppermute(orbitals, "band", across_round)
+    met_next = lax.ppermute(orbitals, "band", next_round)
     before = lax.ppermute(orbitals, "slab", up)
     after = lax.ppermute(orbitals, "slab", down)
-    met_across = lax.ppermute(orbitals, "band", across_round)
-    met_next = lax.ppermute(orbitals, "band", next_round)
 
     weights, partial_value = project(
         entry_slot,
@@ -329,9 +386,9 @@
     applied = apply(orbitals, before, after, potential, beside_all, weights)
 
     volume = 1.0 / (slabs * planes * height * cells)
-    early = gram((orbitals, met_across), orbitals, applied)
-    late = gram((met_next,), orbitals, applied)
-    correlation, subspace = reduce(jnp.concatenate([early, late]) * volume, slabs)
+    early = early_reduce(gram((orbitals, met_across), orbitals, applied) * volume, slabs)
+    late = gram((met_next,), orbitals, applied) * volume
+    correlation, subspace = late_reduce(late, early, slabs)
     return applied, correlation, subspace
 
 

time: 221 us -> 217 us (0.982)
  waiting for transfers between devices: 79.8 us -> 58.5 us
  Pallas kernels: 110 us -> 127 us
  local copies, waits for them, and re-layouts: 13 us -> 8.41 us
    ppermute x1, waiting for transfers between devices: 34.3 us -> 14.6 us  [local(): met_next = lax.ppermute(orbitals, 'band', next_round)]
    pallas_call x1 -> x2, Pallas kernels: 17.4 us -> 27.3 us  [the longest x1 14 us: late_reduce(): pl.pallas_call(functools.partial(late_kernel, slabs), out_shape=(jax.Shap...]
    pallas_call x2, Pallas kernels: 12.2 us -> 20 us  [gram(): pl.pallas_call(functools.partial(gram_kernel, count), grid=(cells // step...]
    unnamed x22 -> x18, local copies, waits for them, and re-layouts: 12.7 us -> 8.14 us
  transfers between devices with their start and end apart: 8 -> 8, of which waited for: 5 -> 5; matrix products, arithmetic and copies ran while one was open for 0% -> 1% of each run, Pallas kernels for 39% -> 49%
where the time goes in v3:
time: 217 us; the launch traced here: 215 us
  Pallas kernels  127 us (59%)
  waiting for transfers between devices  58.5 us (27%)
  starting transfers between devices  17.6 us (8%)
  local copies, waits for them, and re-layouts  8.41 us (4%)
    pallas_call x1, Pallas kernels, project(): pl.pallas_call(functools.partial(project_kernel, slots), out_shape=(jax.S...  41.6 us
    pallas_call x1, Pallas kernels, apply(): pl.pallas_call(apply_kernel, grid=(height,), out_shape=jax.ShapeDtypeStru...  38.5 us
    ppermute x1, waiting for transfers between devices, local(): from_left = lax.ppermute(partial_value[:, 2], 'slab', up)  35.4 us
    pallas_call x2, Pallas kernels, gram(): pl.pallas_call(functools.partial(gram_kernel, count), grid=(cells // step...  20 us
    ppermute x1, waiting for transfers between devices, local(): met_next = lax.ppermute(orbitals, 'band', next_round)  14.6 us
    pallas_call x1, Pallas kernels, late_reduce(): pl.pallas_call(functools.partial(late_kernel, slabs), out_shape=(jax.Shap...  14 us
    pallas_call x1, Pallas kernels, early_reduce(): pl.pallas_call(functools.partial(early_kernel, slabs), out_shape=jax.Shap...  13.3 us
    unnamed x18, local copies, waits for them, and re-layouts  8.14 us
  transfers between devices with their start and end apart: 8, of which 5 were waited for; matrix products, arithmetic and copies ran while one was open for 1% of the time, Pallas kernels for 49%

profile of v3, /device:TPU:0, one launch (start us, length us, event | category | flops | bytes accessed | tf_op | source)
XLA Modules:
  0.0 215.3 jit_solution(17933558948761002963)
XLA Ops:
  0.6 0.5 collective-permute-start
  1.1 2.9 %collective-permute-start.1 = (f32[2,32,128,128]{3,2,1,0:T(8,128)}, f32[2,32,128,128]{3,2,1,0:T(8,128)}, u32[]{:S(2)}, u32[]{:S(2)}) collective-permute-start(f32[2,32,128,128]{3,2,1,0:T(8,128)} %x_ref.1), channel_id=1, source_target_pairs={{4,0},{8,4},{12,8},{16,12},{20,16},{24,20},{28,24},{0,28},{5,1},{9... | collective-permute-start | bytes 12582920 | tf_op jit(solution)/shard_map/ppermute | solution.py:367
  4.1 7.1 %collective-permute-start.7 = (f32[2,32,128,128]{3,2,1,0:T(8,128)}, f32[2,32,128,128]{3,2,1,0:T(8,128)}, u32[]{:S(2)}, u32[]{:S(2)}) collective-permute-start(f32[2,32,128,128]{3,2,1,0:T(8,128)} %x_ref.1), channel_id=1, source_target_pairs={{0,2},{3,1},{4,6},{7,5},{8,10},{11,9},{12,14},{15,13},{16,18},{19,... | collective-permute-start | bytes 12582920 | tf_op jit(solution)/shard_map/ppermute | solution.py:364
  11.2 0.0 collective-permute-start.6
  11.9 2.2 %copy-done = f32[2,32,128,128]{3,2,1,0:T(8,128)S(1)} copy-done((f32[2,32,128,128]{3,2,1,0:T(8,128)S(1)}, f32[2,32,128,128]{3,2,1,0:T(8,128)}, u32[]{:S(2)}) %copy-start) | copy-done | bytes 4194328
  14.1 1.2 copy-done.3
  15.3 0.7 copy-done.4
  16.0 0.7 copy-done.5
  16.7 41.6 %project.1 = (f32[64,768,128]{2,1,0:T(8,128)}, f32[768,128]{1,0:T(8,128)S(1)}) custom-call(s32[512]{0:T(512)S(1)} %copy-done.4, s32[512]{0:T(512)S(1)} %copy-done.5, s32[1]{0:T(128)S(6)} %copy.31.count_ref, f32[512,4,128]{2,1,0:T(4,128)S(1)} %copy-done.3, f32[64,128,128]{2,1,0:T(8,128)S(1)} %bitcast.46), custom_call_target="tpu_custom_call" | custom-call | flops 9663676416 | bytes 25165824 | tf_op jit(solution)/shard_map/project/pallas_call | solution.py:53
  58.3 1.8 collective-permute-start.2
  60.1 35.4 %collective-permute-done.2 = f32[4,64,128]{2,1,0:T(8,128)S(1)} collective-permute-done((f32[4,64,128]{2,1,0:T(8,128)S(1)}, f32[4,64,128]{2,1,0:T(8,128)S(1)}, u32[]{:S(2)}, u32[]{:S(2)}) %collective-permute-start.2) | collective-permute-done | bytes 131104 | tf_op jit(solution)/shard_map/ppermute | solution.py:378
  95.5 2.5 %collective-permute-done.3 = f32[4,64,128]{2,1,0:T(8,128)S(1)} collective-permute-done((f32[4,64,128]{2,1,0:T(8,128)S(1)}, f32[4,64,128]{2,1,0:T(8,128)S(1)}, u32[]{:S(2)}, u32[]{:S(2)}) %collective-permute-start.3) | collective-permute-done | bytes 131104 | tf_op jit(solution)/shard_map/ppermute | solution.py:379
  98.0 0.1 fusion.2
  98.1 2.8 %collective-permute-start.5 = (f32[4,64,128]{2,1,0:T(8,128)S(1)}, f32[4,64,128]{2,1,0:T(8,128)S(1)}, u32[]{:S(2)}, u32[]{:S(2)}) collective-permute-start(f32[4,64,128]{2,1,0:T(8,128)S(1)} %fusion.2), channel_id=1, source_target_pairs={{4,0},{8,4},{12,8},{16,12},{20,16},{24,20},{28,24},{0,28},{5,1},{9... | collective-permute-start | bytes 393224 | tf_op jit(solution)/shard_map/ppermute | solution.py:383
  101.0 2.5 %collective-permute-done.5 = f32[4,64,128]{2,1,0:T(8,128)S(1)} collective-permute-done((f32[4,64,128]{2,1,0:T(8,128)S(1)}, f32[4,64,128]{2,1,0:T(8,128)S(1)}, u32[]{:S(2)}, u32[]{:S(2)}) %collective-permute-start.5) | collective-permute-done | bytes 131104 | tf_op jit(solution)/shard_map/ppermute | solution.py:383
  103.5 2.3 %collective-permute-start.4 = (f32[4,64,128]{2,1,0:T(8,128)S(1)}, f32[4,64,128]{2,1,0:T(8,128)S(1)}, u32[]{:S(2)}, u32[]{:S(2)}) collective-permute-start(f32[4,64,128]{2,1,0:T(8,128)S(1)} %fusion.2), channel_id=1, source_target_pairs={{0,4},{4,8},{8,12},{12,16},{16,20},{20,24},{24,28},{28,0},{1,5},{5... | collective-permute-start | bytes 393224 | tf_op jit(solution)/shard_map/ppermute | solution.py:383
  105.8 3.5 %collective-permute-done.4 = f32[4,64,128]{2,1,0:T(8,128)S(1)} collective-permute-done((f32[4,64,128]{2,1,0:T(8,128)S(1)}, f32[4,64,128]{2,1,0:T(8,128)S(1)}, u32[]{:S(2)}, u32[]{:S(2)}) %collective-permute-start.4) | collective-permute-done | bytes 131104 | tf_op jit(solution)/shard_map/ppermute | solution.py:383
  109.4 0.0 collective-permute-done.1.after_ref
  109.4 2.0 copy-done.6
  111.3 38.5 %apply.1 = f32[2,32,128,128]{3,2,1,0:T(8,128)} custom-call(f32[2,32,128,128]{3,2,1,0:T(8,128)S(1)} %copy-done.1, f32[2,32,128,128]{3,2,1,0:T(8,128)} %copy-done.6, f32[2,32,128,128]{3,2,1,0:T(8,128)} %collective-permute-done.1.after_ref, f32[2,32,128]{2,1,0:T(8,128)S(1)} %copy-done.2, f32[768,128]{1,0:T(8,128)S(1)} %bitcast.47, f32[2,32,768,128]{3,2,1,0:T(8,128)} %bitcast.54), custom_call_target="tpu_custom_call" | custom-call | flops 9663676416 | bytes 25165824 | tf_op jit(solution)/shard_map/apply/pallas_call | solution.py:110
  149.8 0.0 collective-permute-done.7
  149.8 11.3 %gram.3 = f32[256,256]{1,0:T(8,128)} custom-call(f32[8192,128]{1,0:T(8,128)} %bitcast.43, f32[8192,128]{1,0:T(8,128)} %bitcast.18.refs_1_, f32[8192,128]{1,0:T(8,128)} %bitcast.44, f32[8192,128]{1,0:T(8,128)} %bitcast.52), custom_call_target="tpu_custom_call" | custom-call | flops 3221225472 | bytes 16777216 | tf_op jit(solution)/shard_map/gram/pallas_call | solution.py:156
  161.2 1.0 broadcast_multiply_fusion
  162.1 0.1 mul.40
  162.3 13.3 %early_reduce.1.early_ref = f32[2,2,128,128]{3,2,1,0:T(8,128)S(1)} custom-call(f32[8,2,32,128]{3,2,1,0:T(8,128)S(1)} %bitcast.48), custom_call_target="tpu_custom_call" | custom-call | tf_op jit(solution)/shard_map/early_reduce/pallas_call | solution.py:309
  175.6 14.6 %collective-permute-done.6 = f32[2,32,128,128]{3,2,1,0:T(8,128)} collective-permute-done((f32[2,32,128,128]{3,2,1,0:T(8,128)}, f32[2,32,128,128]{3,2,1,0:T(8,128)}, u32[]{:S(2)}, u32[]{:S(2)}) %collective-permute-start.6) | collective-permute-done | bytes 4194336 | tf_op jit(solution)/shard_map/ppermute | solution.py:365
  190.2 8.6 %gram.2 = f32[128,256]{1,0:T(8,128)} custom-call(f32[8192,128]{1,0:T(8,128)} %bitcast.13.refs_0_, f32[8192,128]{1,0:T(8,128)} %bitcast.45, f32[8192,128]{1,0:T(8,128)} %bitcast.53), custom_call_target="tpu_custom_call" | custom-call | flops 1610612736 | bytes 12582912 | tf_op jit(solution)/shard_map/gram/pallas_call | solution.py:156
  198.8 0.9 broadcast_multiply_fusion.1
  199.8 0.1 mul.36
  199.9 14.0 %late_reduce.1 = (f32[512,128]{1,0:T(8,128)S(1)}, f32[512,128]{1,0:T(8,128)S(1)}) custom-call(f32[8,1,32,128]{3,2,1,0:T(8,128)S(1)} %bitcast.49, f32[2,2,128,128]{3,2,1,0:T(8,128)S(1)} %early_reduce.1.early_ref), custom_call_target="tpu_custom_call" | custom-call | tf_op jit(solution)/shard_map/late_reduce/pallas_call | solution.py:331
  213.9 0.7 copy.32
  214.6 0.7 copy.33
  (18 shorter events, 0.1 us)
Async XLA Ops:
  0.6 108.7 %collective-permute-start = (f32[2,32,128,128]{3,2,1,0:T(8,128)}, f32[2,32,128,128]{3,2,1,0:T(8,128)S(1)}, u32[]{:S(2)}, u32[]{:S(2)}) collective-permute-start(f32[2,32,128,128]{3,2,1,0:T(8,128)} %x_ref.1), channel_id=1, source_target_pairs={{0,4},{4,8},{8,12},{12,16},{16,20},{20,24},{24,28},{28,0},{1,5},{5... | collective-permute-start | bytes 12582920 | tf_op jit(solution)/shard_map/ppermute | solution.py:366
  1.1 108.2 %collective-permute-start.1 = (f32[2,32,128,128]{3,2,1,0:T(8,128)}, f32[2,32,128,128]{3,2,1,0:T(8,128)}, u32[]{:S(2)}, u32[]{:S(2)}) collective-permute-start(f32[2,32,128,128]{3,2,1,0:T(8,128)} %x_ref.1), channel_id=1, source_target_pairs={{4,0},{8,4},{12,8},{16,12},{20,16},{24,20},{28,24},{0,28},{5,1},{9... | collective-permute-start | bytes 12582920 | tf_op jit(solution)/shard_map/ppermute | solution.py:367
  4.1 145.7 %collective-permute-start.7 = (f32[2,32,128,128]{3,2,1,0:T(8,128)}, f32[2,32,128,128]{3,2,1,0:T(8,128)}, u32[]{:S(2)}, u32[]{:S(2)}) collective-permute-start(f32[2,32,128,128]{3,2,1,0:T(8,128)} %x_ref.1), channel_id=1, source_target_pairs={{0,2},{3,1},{4,6},{7,5},{8,10},{11,9},{12,14},{15,13},{16,18},{19,... | collective-permute-start | bytes 12582920 | tf_op jit(solution)/shard_map/ppermute | solution.py:364
  11.2 179.0 %collective-permute-start.6 = (f32[2,32,128,128]{3,2,1,0:T(8,128)}, f32[2,32,128,128]{3,2,1,0:T(8,128)}, u32[]{:S(2)}, u32[]{:S(2)}) collective-permute-start(f32[2,32,128,128]{3,2,1,0:T(8,128)} %x_ref.1), channel_id=1, source_target_pairs={{0,1},{1,2},{2,3},{3,0},{4,5},{5,6},{6,7},{7,4},{8,9},{9,10},{10,1... | collective-permute-start | bytes 12582920 | tf_op jit(solution)/shard_map/ppermute | solution.py:365
  11.9 2.2 %copy-start = (f32[2,32,128,128]{3,2,1,0:T(8,128)S(1)}, f32[2,32,128,128]{3,2,1,0:T(8,128)}, u32[]{:S(2)}) copy-start(f32[2,32,128,128]{3,2,1,0:T(8,128)} %x_ref.1) | copy-start | bytes 12582916
  14.1 1.2 copy-start.3
  15.3 0.7 copy-start.4
  16.0 0.7 copy-start.5
  16.6 81.4 %copy-start.7 = (f32[64,4]{0,1:T(4,128)S(1)}, f32[64,4]{0,1:T(4,128)}, u32[]{:S(2)}) copy-start(f32[64,4]{0,1:T(4,128)} %param.10) | copy-start | bytes 3076
  16.6 94.7 %copy-start.1 = (f32[2,32,128,128]{3,2,1,0:T(8,128)S(1)}, f32[2,32,128,128]{3,2,1,0:T(8,128)}, u32[]{:S(2)}) copy-start(f32[2,32,128,128]{3,2,1,0:T(8,128)} %x_ref.1) | copy-start | bytes 12582916
  16.7 94.7 %copy-start.2 = (f32[2,32,128]{2,1,0:T(8,128)S(1)}, f32[2,32,128]{2,1,0:T(8,128)}, u32[]{:S(2)}) copy-start(f32[2,32,128]{2,1,0:T(8,128)} %potential_ref.1) | copy-start | bytes 98308
  58.3 37.2 %collective-permute-start.2 = (f32[4,64,128]{2,1,0:T(8,128)S(1)}, f32[4,64,128]{2,1,0:T(8,128)S(1)}, u32[]{:S(2)}, u32[]{:S(2)}) collective-permute-start(f32[4,64,128]{2,1,0:T(8,128)S(1)} %get-tuple-element.11), channel_id=1, source_target_pairs={{0,4},{4,8},{8,12},{12,16},{16,20},{20,24},{24,28},{28,0},{1,5},{5... | collective-permute-start | bytes 393224 | tf_op jit(solution)/shard_map/ppermute | solution.py:378
  95.5 2.5 %collective-permute-start.3 = (f32[4,64,128]{2,1,0:T(8,128)S(1)}, f32[4,64,128]{2,1,0:T(8,128)S(1)}, u32[]{:S(2)}, u32[]{:S(2)}) collective-permute-start(f32[4,64,128]{2,1,0:T(8,128)S(1)} %get-tuple-element.12), channel_id=1, source_target_pairs={{4,0},{8,4},{12,8},{16,12},{20,16},{24,20},{28,24},{0,28},{5,1},{9... | collective-permute-start | bytes 393224 | tf_op jit(solution)/shard_map/ppermute | solution.py:379
  98.1 5.3 %collective-permute-start.5 = (f32[4,64,128]{2,1,0:T(8,128)S(1)}, f32[4,64,128]{2,1,0:T(8,128)S(1)}, u32[]{:S(2)}, u32[]{:S(2)}) collective-permute-start(f32[4,64,128]{2,1,0:T(8,128)S(1)} %fusion.2), channel_id=1, source_target_pairs={{4,0},{8,4},{12,8},{16,12},{20,16},{24,20},{28,24},{0,28},{5,1},{9... | collective-permute-start | bytes 393224 | tf_op jit(solution)/shard_map/ppermute | solution.py:383
  103.5 5.8 %collective-permute-start.4 = (f32[4,64,128]{2,1,0:T(8,128)S(1)}, f32[4,64,128]{2,1,0:T(8,128)S(1)}, u32[]{:S(2)}, u32[]{:S(2)}) collective-permute-start(f32[4,64,128]{2,1,0:T(8,128)S(1)} %fusion.2), channel_id=1, source_target_pairs={{0,4},{4,8},{8,12},{12,16},{16,20},{20,24},{24,28},{28,0},{1,5},{5... | collective-permute-start | bytes 393224 | tf_op jit(solution)/shard_map/ppermute | solution.py:383
  109.4 2.0 copy-start.6

commit v4 on v3

--- a/solution.py
+++ b/solution.py
@@ -123,8 +123,9 @@
     )(orbitals, before, after, potential, scaled, weights.reshape(planes, height, depth, cells))
 
 
-def gram_kernel(count, *refs):
-    *left_refs, x_ref, applied_ref, out_ref = refs
+def gram_kernel(count, scale, *refs):
+    *left_refs, x_ref, applied_ref, out_ref, total = refs
+    cols = x_ref.shape[1]
     bf16 = jnp.bfloat16
 
     def halves(values):
@@ -138,27 +139,36 @@
 
     @pl.when(pl.program_id(0) == 0)
     def _():
-        out_ref[...] = jnp.zeros_like(out_ref)
+        total[...] = jnp.zeros_like(total)
 
     left_high, left_low = halves(jnp.concatenate([ref[...] for ref in left_refs], axis=1))
     right_high, right_low = halves(jnp.concatenate([x_ref[...], applied_ref[...]], axis=1))
-    out_ref[...] += (
-        times(left_high, right_high) + times(left_high, right_low) + times(left_low, right_high)
-    )
-
-
-def gram(lefts, orbitals, applied):
+    both = times(jnp.concatenate([left_high, left_low], axis=1), right_high)
+    depth = count * cols
+    total[...] += both[:depth] + both[depth:] + times(left_high, right_low)
+
+    @pl.when(pl.program_id(0) == pl.num_programs(0) - 1)
+    def _():
+        for left in range(count):
+            for right in range(2):
+                out_ref[left, right] = scale * total[
+                    left * cols : (left + 1) * cols, right * cols : (right + 1) * cols
+                ]
+
+
+def gram(lefts, orbitals, applied, scale):
     cols = orbitals.shape[-1]
     cells = orbitals.size // cols
     step = min(1024, cells)
     arrays = [x.reshape(cells, cols) for x in (*lefts, orbitals, applied)]
     count = len(lefts)
-    out = pl.pallas_call(
-        functools.partial(gram_kernel, count),
+    return pl.pallas_call(
+        functools.partial(gram_kernel, count, scale),
         grid=(cells // step,),
-        out_shape=jax.ShapeDtypeStruct((count * cols, 2 * cols), jnp.float32),
+        out_shape=jax.ShapeDtypeStruct((count, 2, cols, cols), jnp.float32),
         in_specs=[pl.BlockSpec((step, cols), lambda i: (i, 0))] * len(arrays),
-        out_specs=pl.BlockSpec((count * cols, 2 * cols), lambda i: (0, 0)),
+        out_specs=pl.BlockSpec((count, 2, cols, cols), lambda i: (0, 0, 0, 0)),
+        scratch_shapes=[pltpu.VMEM((count * cols, 2 * cols), jnp.float32)],
         compiler_params=pltpu.CompilerParams(vmem_limit_bytes=60 * MIB),
         cost_estimate=pl.CostEstimate(
             flops=12 * count * cells * cols * cols,
@@ -167,7 +177,6 @@
         ),
         name="gram",
     )(*arrays)
-    return jnp.swapaxes(out.reshape(count, cols, 2, cols), 1, 2)
 
 
 mesh_type = pl.DeviceIdType.MESH
@@ -386,8 +395,8 @@
     applied = apply(orbitals, before, after, potential, beside_all, weights)
 
     volume = 1.0 / (slabs * planes * height * cells)
-    early = early_reduce(gram((orbitals, met_across), orbitals, applied) * volume, slabs)
-    late = gram((met_next,), orbitals, applied) * volume
+    early = early_reduce(gram((orbitals, met_across), orbitals, applied, volume), slabs)
+    late = gram((met_next,), orbitals, applied, volume)
     correlation, subspace = late_reduce(late, early, slabs)
     return applied, correlation, subspace
 

time: 217 us -> 217 us (level)
  waiting for transfers between devices: 58.5 us -> 61.1 us
    ppermute x1, waiting for transfers between devices: 35.4 us -> 37.8 us  [local(): from_left = lax.ppermute(partial_value[:, 2], 'slab', up)]
    unnamed x18 -> x20, local copies, waits for them, and re-layouts: 8.14 us -> 9.05 us
  transfers between devices with their start and end apart: 8 -> 8, of which waited for: 5 -> 5; matrix products, arithmetic and copies ran while one was open for 1% -> 1% of each run, Pallas kernels for 49% -> 48%
where the time goes in v4:
time: 217 us; the launch traced here: 215 us
  Pallas kernels  126 us (58%)
  waiting for transfers between devices  61.1 us (28%)
  starting transfers between devices  16.2 us (7%)
  local copies, waits for them, and re-layouts  10 us (5%)
    pallas_call x1, Pallas kernels, project(): pl.pallas_call(functools.partial(project_kernel, slots), out_shape=(jax.S...  40.5 us
    pallas_call x1, Pallas kernels, apply(): pl.pallas_call(apply_kernel, grid=(height,), out_shape=jax.ShapeDtypeStru...  38.5 us
    ppermute x1, waiting for transfers between devices, local(): from_left = lax.ppermute(partial_value[:, 2], 'slab', up)  37.8 us
    pallas_call x2, Pallas kernels, gram(): pl.pallas_call(functools.partial(gram_kernel, count, scale), grid=(cells...  20.1 us
    ppermute x1, waiting for transfers between devices, local(): met_next = lax.ppermute(orbitals, 'band', next_round)  14.8 us
    pallas_call x1, Pallas kernels, late_reduce(): pl.pallas_call(functools.partial(late_kernel, slabs), out_shape=(jax.Shap...  13.9 us
    pallas_call x1, Pallas kernels, early_reduce(): pl.pallas_call(functools.partial(early_kernel, slabs), out_shape=jax.Shap...  13.3 us
    unnamed x20, local copies, waits for them, and re-layouts  9.05 us
  transfers between devices with their start and end apart: 8, of which 5 were waited for; matrix products, arithmetic and copies ran while one was open for 1% of the time, Pallas kernels for 48%

profile of v4, /device:TPU:0, one launch (start us, length us, event | category | flops | bytes accessed | tf_op | source)
XLA Modules:
  0.0 215.2 jit_solution(15230163496803722168)
XLA Ops:
  0.6 0.5 collective-permute-start
  1.1 2.9 %collective-permute-start.1 = (f32[2,32,128,128]{3,2,1,0:T(8,128)}, f32[2,32,128,128]{3,2,1,0:T(8,128)}, u32[]{:S(2)}, u32[]{:S(2)}) collective-permute-start(f32[2,32,128,128]{3,2,1,0:T(8,128)} %x_ref.1), channel_id=1, source_target_pairs={{4,0},{8,4},{12,8},{16,12},{20,16},{24,20},{28,24},{0,28},{5,1},{9... | collective-permute-start | bytes 12582920 | tf_op jit(solution)/shard_map/ppermute | solution.py:376
  4.1 7.1 %collective-permute-start.7 = (f32[2,32,128,128]{3,2,1,0:T(8,128)}, f32[2,32,128,128]{3,2,1,0:T(8,128)}, u32[]{:S(2)}, u32[]{:S(2)}) collective-permute-start(f32[2,32,128,128]{3,2,1,0:T(8,128)} %x_ref.1), channel_id=1, source_target_pairs={{0,2},{3,1},{4,6},{7,5},{8,10},{11,9},{12,14},{15,13},{16,18},{19,... | collective-permute-start | bytes 12582920 | tf_op jit(solution)/shard_map/ppermute | solution.py:373
  11.2 0.0 collective-permute-start.6
  11.9 2.2 %copy-done = f32[2,32,128,128]{3,2,1,0:T(8,128)S(1)} copy-done((f32[2,32,128,128]{3,2,1,0:T(8,128)S(1)}, f32[2,32,128,128]{3,2,1,0:T(8,128)}, u32[]{:S(2)}) %copy-start) | copy-done | bytes 4194328
  14.1 1.2 copy-done.4
  15.3 0.7 copy-done.5
  16.0 0.7 copy-done.6
  16.7 40.5 %project.1 = (f32[64,768,128]{2,1,0:T(8,128)}, f32[768,128]{1,0:T(8,128)S(1)}) custom-call(s32[512]{0:T(512)S(1)} %copy-done.5, s32[512]{0:T(512)S(1)} %copy-done.6, s32[1]{0:T(128)S(6)} %copy.28.count_ref, f32[512,4,128]{2,1,0:T(4,128)S(1)} %copy-done.4, f32[64,128,128]{2,1,0:T(8,128)S(1)} %bitcast.42), custom_call_target="tpu_custom_call" | custom-call | flops 9663676416 | bytes 25165824 | tf_op jit(solution)/shard_map/project/pallas_call | solution.py:53
  57.2 0.5 collective-permute-start.2
  57.7 37.8 %collective-permute-done.2 = f32[4,64,128]{2,1,0:T(8,128)S(1)} collective-permute-done((f32[4,64,128]{2,1,0:T(8,128)S(1)}, f32[4,64,128]{2,1,0:T(8,128)S(1)}, u32[]{:S(2)}, u32[]{:S(2)}) %collective-permute-start.2) | collective-permute-done | bytes 131104 | tf_op jit(solution)/shard_map/ppermute | solution.py:387
  95.5 0.0 collective-permute-start.3
  95.5 2.5 %collective-permute-done.3 = f32[4,64,128]{2,1,0:T(8,128)S(1)} collective-permute-done((f32[4,64,128]{2,1,0:T(8,128)S(1)}, f32[4,64,128]{2,1,0:T(8,128)S(1)}, u32[]{:S(2)}, u32[]{:S(2)}) %collective-permute-start.3) | collective-permute-done | bytes 131104 | tf_op jit(solution)/shard_map/ppermute | solution.py:388
  98.0 0.1 fusion.2
  98.1 2.8 %collective-permute-start.5 = (f32[4,64,128]{2,1,0:T(8,128)S(1)}, f32[4,64,128]{2,1,0:T(8,128)S(1)}, u32[]{:S(2)}, u32[]{:S(2)}) collective-permute-start(f32[4,64,128]{2,1,0:T(8,128)S(1)} %fusion.2), channel_id=1, source_target_pairs={{4,0},{8,4},{12,8},{16,12},{20,16},{24,20},{28,24},{0,28},{5,1},{9... | collective-permute-start | bytes 393224 | tf_op jit(solution)/shard_map/ppermute | solution.py:392
  101.0 2.5 %collective-permute-done.5 = f32[4,64,128]{2,1,0:T(8,128)S(1)} collective-permute-done((f32[4,64,128]{2,1,0:T(8,128)S(1)}, f32[4,64,128]{2,1,0:T(8,128)S(1)}, u32[]{:S(2)}, u32[]{:S(2)}) %collective-permute-start.5) | collective-permute-done | bytes 131104 | tf_op jit(solution)/shard_map/ppermute | solution.py:392
  103.5 2.3 %collective-permute-start.4 = (f32[4,64,128]{2,1,0:T(8,128)S(1)}, f32[4,64,128]{2,1,0:T(8,128)S(1)}, u32[]{:S(2)}, u32[]{:S(2)}) collective-permute-start(f32[4,64,128]{2,1,0:T(8,128)S(1)} %fusion.2), channel_id=1, source_target_pairs={{0,4},{4,8},{8,12},{12,16},{16,20},{20,24},{24,28},{28,0},{1,5},{5... | collective-permute-start | bytes 393224 | tf_op jit(solution)/shard_map/ppermute | solution.py:392
  105.8 3.5 %collective-permute-done.4 = f32[4,64,128]{2,1,0:T(8,128)S(1)} collective-permute-done((f32[4,64,128]{2,1,0:T(8,128)S(1)}, f32[4,64,128]{2,1,0:T(8,128)S(1)}, u32[]{:S(2)}, u32[]{:S(2)}) %collective-permute-start.4) | collective-permute-done | bytes 131104 | tf_op jit(solution)/shard_map/ppermute | solution.py:392
  109.3 0.0 collective-permute-done.before_ref
  109.4 0.0 collective-permute-done.1.after_ref
  109.4 2.0 copy-done.7
  111.3 38.5 %apply.1 = f32[2,32,128,128]{3,2,1,0:T(8,128)} custom-call(f32[2,32,128,128]{3,2,1,0:T(8,128)S(1)} %copy-done.1, f32[2,32,128,128]{3,2,1,0:T(8,128)} %copy-done.7, f32[2,32,128,128]{3,2,1,0:T(8,128)} %collective-permute-done.1.after_ref, f32[2,32,128]{2,1,0:T(8,128)S(1)} %copy-done.3, f32[768,128]{1,0:T(8,128)S(1)} %bitcast.43, f32[2,32,768,128]{3,2,1,0:T(8,128)} %bitcast.50), custom_call_target="tpu_custom_call" | custom-call | flops 9663676416 | bytes 25165824 | tf_op jit(solution)/shard_map/apply/pallas_call | solution.py:110
  149.8 0.0 collective-permute-done.7
  149.8 11.3 %gram.3 = f32[2,2,128,128]{3,2,1,0:T(8,128)} custom-call(f32[8192,128]{1,0:T(8,128)} %bitcast.39, f32[8192,128]{1,0:T(8,128)} %bitcast.17.refs_1_, f32[8192,128]{1,0:T(8,128)} %bitcast.40, f32[8192,128]{1,0:T(8,128)} %bitcast.48), custom_call_target="tpu_custom_call" | custom-call | flops 3221225472 | bytes 16777216 | tf_op jit(solution)/shard_map/gram/pallas_call | solution.py:165
  161.2 1.0 copy.25
  162.1 13.3 %early_reduce.1.early_ref = f32[2,2,128,128]{3,2,1,0:T(8,128)S(1)} custom-call(f32[8,2,32,128]{3,2,1,0:T(8,128)S(1)} %bitcast.44), custom_call_target="tpu_custom_call" | custom-call | tf_op jit(solution)/shard_map/early_reduce/pallas_call | solution.py:318
  175.4 14.8 %collective-permute-done.6 = f32[2,32,128,128]{3,2,1,0:T(8,128)} collective-permute-done((f32[2,32,128,128]{3,2,1,0:T(8,128)}, f32[2,32,128,128]{3,2,1,0:T(8,128)}, u32[]{:S(2)}, u32[]{:S(2)}) %collective-permute-start.6) | collective-permute-done | bytes 4194336 | tf_op jit(solution)/shard_map/ppermute | solution.py:374
  190.2 8.8 %gram.2 = f32[1,2,128,128]{3,2,1,0:T(8,128)} custom-call(f32[8192,128]{1,0:T(8,128)} %bitcast.13.refs_0_, f32[8192,128]{1,0:T(8,128)} %bitcast.41, f32[8192,128]{1,0:T(8,128)} %bitcast.49), custom_call_target="tpu_custom_call" | custom-call | flops 1610612736 | bytes 12582912 | tf_op jit(solution)/shard_map/gram/pallas_call | solution.py:165
  199.0 0.9 copy-done.2
  199.9 13.9 %late_reduce.1 = (f32[512,128]{1,0:T(8,128)S(1)}, f32[512,128]{1,0:T(8,128)S(1)}) custom-call(f32[8,1,32,128]{3,2,1,0:T(8,128)S(1)} %bitcast.45, f32[2,2,128,128]{3,2,1,0:T(8,128)S(1)} %early_reduce.1.early_ref), custom_call_target="tpu_custom_call" | custom-call | tf_op jit(solution)/shard_map/late_reduce/pallas_call | solution.py:340
  213.8 0.7 copy.29
  214.5 0.7 copy.30
  (14 shorter events, 0.1 us)
Async XLA Ops:
  0.6 108.7 %collective-permute-start = (f32[2,32,128,128]{3,2,1,0:T(8,128)}, f32[2,32,128,128]{3,2,1,0:T(8,128)S(1)}, u32[]{:S(2)}, u32[]{:S(2)}) collective-permute-start(f32[2,32,128,128]{3,2,1,0:T(8,128)} %x_ref.1), channel_id=1, source_target_pairs={{0,4},{4,8},{8,12},{12,16},{16,20},{20,24},{24,28},{28,0},{1,5},{5... | collective-permute-start | bytes 12582920 | tf_op jit(solution)/shard_map/ppermute | solution.py:375
  1.1 108.2 %collective-permute-start.1 = (f32[2,32,128,128]{3,2,1,0:T(8,128)}, f32[2,32,128,128]{3,2,1,0:T(8,128)}, u32[]{:S(2)}, u32[]{:S(2)}) collective-permute-start(f32[2,32,128,128]{3,2,1,0:T(8,128)} %x_ref.1), channel_id=1, source_target_pairs={{4,0},{8,4},{12,8},{16,12},{20,16},{24,20},{28,24},{0,28},{5,1},{9... | collective-permute-start | bytes 12582920 | tf_op jit(solution)/shard_map/ppermute | solution.py:376
  4.1 145.8 %collective-permute-start.7 = (f32[2,32,128,128]{3,2,1,0:T(8,128)}, f32[2,32,128,128]{3,2,1,0:T(8,128)}, u32[]{:S(2)}, u32[]{:S(2)}) collective-permute-start(f32[2,32,128,128]{3,2,1,0:T(8,128)} %x_ref.1), channel_id=1, source_target_pairs={{0,2},{3,1},{4,6},{7,5},{8,10},{11,9},{12,14},{15,13},{16,18},{19,... | collective-permute-start | bytes 12582920 | tf_op jit(solution)/shard_map/ppermute | solution.py:373
  11.2 179.0 %collective-permute-start.6 = (f32[2,32,128,128]{3,2,1,0:T(8,128)}, f32[2,32,128,128]{3,2,1,0:T(8,128)}, u32[]{:S(2)}, u32[]{:S(2)}) collective-permute-start(f32[2,32,128,128]{3,2,1,0:T(8,128)} %x_ref.1), channel_id=1, source_target_pairs={{0,1},{1,2},{2,3},{3,0},{4,5},{5,6},{6,7},{7,4},{8,9},{9,10},{10,1... | collective-permute-start | bytes 12582920 | tf_op jit(solution)/shard_map/ppermute | solution.py:374
  11.9 2.2 %copy-start = (f32[2,32,128,128]{3,2,1,0:T(8,128)S(1)}, f32[2,32,128,128]{3,2,1,0:T(8,128)}, u32[]{:S(2)}) copy-start(f32[2,32,128,128]{3,2,1,0:T(8,128)} %x_ref.1) | copy-start | bytes 12582916
  14.1 1.2 copy-start.4
  15.3 0.7 copy-start.5
  16.0 0.7 copy-start.6
  16.7 81.4 %copy-start.8 = (f32[64,4]{0,1:T(4,128)S(1)}, f32[64,4]{0,1:T(4,128)}, u32[]{:S(2)}) copy-start(f32[64,4]{0,1:T(4,128)} %param.10) | copy-start | bytes 3076
  16.7 94.7 %copy-start.1 = (f32[2,32,128,128]{3,2,1,0:T(8,128)S(1)}, f32[2,32,128,128]{3,2,1,0:T(8,128)}, u32[]{:S(2)}) copy-start(f32[2,32,128,128]{3,2,1,0:T(8,128)} %x_ref.1) | copy-start | bytes 12582916
  16.7 94.7 %copy-start.3 = (f32[2,32,128]{2,1,0:T(8,128)S(1)}, f32[2,32,128]{2,1,0:T(8,128)}, u32[]{:S(2)}) copy-start(f32[2,32,128]{2,1,0:T(8,128)} %potential_ref.1) | copy-start | bytes 98308
  57.2 38.3 %collective-permute-start.2 = (f32[4,64,128]{2,1,0:T(8,128)S(1)}, f32[4,64,128]{2,1,0:T(8,128)S(1)}, u32[]{:S(2)}, u32[]{:S(2)}) collective-permute-start(f32[4,64,128]{2,1,0:T(8,128)S(1)} %get-tuple-element.11), channel_id=1, source_target_pairs={{0,4},{4,8},{8,12},{12,16},{16,20},{20,24},{24,28},{28,0},{1,5},{5... | collective-permute-start | bytes 393224 | tf_op jit(solution)/shard_map/ppermute | solution.py:387
  95.5 2.5 %collective-permute-start.3 = (f32[4,64,128]{2,1,0:T(8,128)S(1)}, f32[4,64,128]{2,1,0:T(8,128)S(1)}, u32[]{:S(2)}, u32[]{:S(2)}) collective-permute-start(f32[4,64,128]{2,1,0:T(8,128)S(1)} %get-tuple-element.12), channel_id=1, source_target_pairs={{4,0},{8,4},{12,8},{16,12},{20,16},{24,20},{28,24},{0,28},{5,1},{9... | collective-permute-start | bytes 393224 | tf_op jit(solution)/shard_map/ppermute | solution.py:388
  98.1 5.3 %collective-permute-start.5 = (f32[4,64,128]{2,1,0:T(8,128)S(1)}, f32[4,64,128]{2,1,0:T(8,128)S(1)}, u32[]{:S(2)}, u32[]{:S(2)}) collective-permute-start(f32[4,64,128]{2,1,0:T(8,128)S(1)} %fusion.2), channel_id=1, source_target_pairs={{4,0},{8,4},{12,8},{16,12},{20,16},{24,20},{28,24},{0,28},{5,1},{9... | collective-permute-start | bytes 393224 | tf_op jit(solution)/shard_map/ppermute | solution.py:392
  103.5 5.8 %collective-permute-start.4 = (f32[4,64,128]{2,1,0:T(8,128)S(1)}, f32[4,64,128]{2,1,0:T(8,128)S(1)}, u32[]{:S(2)}, u32[]{:S(2)}) collective-permute-start(f32[4,64,128]{2,1,0:T(8,128)S(1)} %fusion.2), channel_id=1, source_target_pairs={{0,4},{4,8},{8,12},{12,16},{16,20},{20,24},{24,28},{28,0},{1,5},{5... | collective-permute-start | bytes 393224 | tf_op jit(solution)/shard_map/ppermute | solution.py:392
  109.4 2.0 copy-start.7
  199.0 0.9 copy-start.2
